TPU v7x, 256 devices: a whole 4x4x8 slice. The times are simulated.
256 devices in a mesh: group: 16 (over y, x), index: 8 (over z), tensor: 2 (over core).
Axes of the slice: x: 4, y: 4, z: 8, core: 2. Of those that a mesh axis runs over, the one named last changes fastest.
Arguments:
- queries: bfloat16 [16384, 4096], P(('group', 'index'), 'tensor'), may hold values from -4 to 4
- passages: bfloat16 [65536, 4096], P(('group', 'index'), 'tensor'), may hold values from -4 to 4
- positive_slot: int32 [16384], P(('group', 'index')), may hold values from 0 to 511
- hard_offset: int32 [16384, 7], P(('group', 'index')), may hold values from 0 to 6, as said below
- hard_slot: int32 [16384, 7], P(('group', 'index')), may hold values from 0 to 511
Outputs:
- loss: float32 [], replicated
- query_grad: bfloat16 [16384, 4096], P(('group', 'index'), 'tensor')
- passage_grad: bfloat16 [65536, 4096], P(('group', 'index'), 'tensor')
Inputs may be any that keep to these rules, and one draw needn't show every extreme that they name: `hard_offset`: within one block's rows, one offset is named exactly 192 times and the other offsets share the remaining 128 * 7 - 192 entries evenly, their counts differing by at most one; which offset is the busy one varies by block.
All inputs are finite; a program needn't handle non-finite values.
Results may differ from a plain program's by a relative error of at most 0.008.
Values may be sent and summed in bfloat16 or wider, within the bound.
A program may use at most 128 MiB of HBM per device.

v0:
```python
import jax
import jax.numpy as jnp
from jax import lax
from jax.sharding import PartitionSpec as P

epsilon = 1e-06
inverse_temp = 50.0


def softmax_terms(score_in, score_hard, first_row, row_count):
    scaled_in = inverse_temp * score_in
    scaled_hard = inverse_temp * score_hard
    log_total = jnp.log(jnp.sum(jnp.exp(scaled_in), axis=1) + jnp.sum(jnp.exp(scaled_hard), axis=1))
    columns_now = jnp.arange(scaled_in.shape[1], dtype=jnp.int32)[None, :]
    own_columns = first_row + jnp.arange(row_count, dtype=jnp.int32)[:, None]
    target = (columns_now == own_columns).astype(jnp.float32)
    loss_part = jnp.sum(log_total - jnp.sum(scaled_in * target, axis=1))
    weight_in = (inverse_temp * (jnp.exp(scaled_in - log_total[:, None]) - target)).astype(
        jnp.bfloat16
    )
    weight_hard = (inverse_temp * jnp.exp(scaled_hard - log_total[:, None])).astype(jnp.bfloat16)
    return (weight_in, weight_hard, loss_part)


def on_device(queries, passages, positive_slot, hard_offset, hard_slot):
    q_rows, width = queries.shape
    p_rows = passages.shape[0]
    negatives = hard_offset.shape[1]
    groups = lax.axis_size("group")
    owners = lax.axis_size("index")
    capacity = (3 * q_rows * negatives // (2 * (owners - 1)) + 7) // 8 * 8
    query_wide = queries.astype(jnp.float32)
    passage_wide = passages.astype(jnp.float32)
    query_squares, passage_squares = lax.psum(
        (jnp.sum(query_wide * query_wide, axis=1), jnp.sum(passage_wide * passage_wide, axis=1)),
        "tensor",
    )
    query_norm = jnp.sqrt(query_squares + epsilon)[:, None]
    passage_norm = jnp.sqrt(passage_squares + epsilon)[:, None]
    unit_query = query_wide / query_norm
    query_hat = unit_query.astype(jnp.bfloat16)
    unit_passage = passage_wide / passage_norm
    passage_hat = unit_passage.astype(jnp.bfloat16)
    positive_rows = passage_hat[positive_slot]
    batch_block = lax.all_gather(positive_rows, "group", axis=0, tiled=True)
    own_index = lax.axis_index("index")
    owner_ids = ((own_index + 1 + hard_offset) % owners).reshape(-1)
    flat_slots = hard_slot.reshape(-1)
    owner_hits = (owner_ids[:, None] == jnp.arange(owners, dtype=jnp.int32)[None, :]).astype(
        jnp.int32
    )
    position = jnp.sum((jnp.cumsum(owner_hits, axis=0) - 1) * owner_hits, axis=1)
    requests = jnp.zeros((owners, capacity), jnp.int32).at[owner_ids, position].set(flat_slots)
    asked_slots = lax.all_to_all(requests, "index", split_axis=0, concat_axis=0, tiled=True)
    fetched = passage_hat[asked_slots]
    answered, asked_slots = (
        lax.all_to_all(fetched, "index", split_axis=0, concat_axis=0, tiled=True),
        asked_slots,
    )
    hard_rows = answered[owner_ids, position].reshape(q_rows, negatives, width)
    part_in = lax.dot_general(
        query_hat, batch_block, (((1,), (1,)), ((), ())), preferred_element_type=jnp.float32
    )
    part_hard = jnp.einsum("qd,qjd->qj", query_hat, hard_rows, preferred_element_type=jnp.float32)
    column_base = lax.axis_index("group") * q_rows
    score_in, score_hard = lax.psum((part_in, part_hard), "tensor")
    weight_in, weight_hard, loss_part = softmax_terms(score_in, score_hard, column_base, q_rows)
    summed_loss = lax.psum(loss_part, ("group", "index"))
    loss = summed_loss / (q_rows * groups * owners)
    query_hat_grad = jnp.dot(weight_in, batch_block, preferred_element_type=jnp.float32)
    query_hat_grad = query_hat_grad + jnp.einsum(
        "qj,qjd->qd", weight_hard, hard_rows, preferred_element_type=jnp.float32
    )
    weight_columns = lax.all_to_all(weight_in, "group", split_axis=1, concat_axis=0, tiled=True)
    positive_grad = lax.dot_general(
        weight_columns,
        lax.all_gather(query_hat, "group", axis=0, tiled=True),
        (((0,), (0,)), ((), ())),
        preferred_element_type=jnp.float32,
    )
    passage_hat_grad = jnp.zeros((p_rows, width), jnp.float32).at[positive_slot].add(positive_grad)
    hard_grad = (
        weight_hard.astype(jnp.float32)[:, :, None] * query_hat.astype(jnp.float32)[:, None, :]
    ).astype(jnp.bfloat16)
    outgoing = (
        jnp.zeros((owners, capacity, width), jnp.bfloat16)
        .at[owner_ids, position]
        .set(hard_grad.reshape(q_rows * negatives, width))
    )
    returned = lax.all_to_all(outgoing, "index", split_axis=0, concat_axis=0, tiled=True)
    passage_hat_grad = passage_hat_grad.at[asked_slots.reshape(-1)].add(
        returned.reshape(owners * capacity, width).astype(jnp.float32)
    )
    query_along, passage_along = lax.psum(
        (
            jnp.sum(unit_query * query_hat_grad, axis=1),
            jnp.sum(unit_passage * passage_hat_grad, axis=1),
        ),
        "tensor",
    )
    query_grad = ((query_hat_grad - unit_query * query_along[:, None]) / query_norm).astype(
        jnp.bfloat16
    )
    passage_grad = (
        (passage_hat_grad - unit_passage * passage_along[:, None]) / passage_norm
    ).astype(jnp.bfloat16)
    return (loss, query_grad, passage_grad)


def solution(mesh):
    in_specs = (
        P(("group", "index"), "tensor"),
        P(("group", "index"), "tensor"),
        P(("group", "index")),
        P(("group", "index"), None),
        P(("group", "index"), None),
    )
    out_specs = (P(), P(("group", "index"), "tensor"), P(("group", "index"), "tensor"))
    return jax.shard_map(
        on_device, mesh=mesh, in_specs=in_specs, out_specs=out_specs, check_vma=False
    )
```

profile of v0, /device:TPU:1, one launch (start us, length us, event | category | flops | bytes accessed | tf_op | source)
XLA Modules:
  0.0 1000.6 jit_solution(17808636137094612035)
XLA Ops:
  10.5 5.4 all-reduce.1
  23.8 45.0 %scatter_fusion = s32[8,192]{1,0:T(8,128)S(1)} fusion(s32[8,192]{1,0:T(8,128)S(1)} %broadcast.127, s32[896]{0:T(1024)S(1)} %get-tuple-element.6, s32[896]{0:T(1024)S(1)} %reshape.196), kind=kCustom, calls=%fused_computation.3 | custom fusion | bytes 17920 | tf_op jit(solution)/shard_map/scatter | solution.py:53
  68.8 12.8 %all_to_all.41 = s32[8,1,192]{2,1,0:T(1,128)S(1)} all-to-all(s32[8,1,192]{2,1,0:T(1,128)S(1)} %copy.31), channel_id=1, replica_groups=mesh['group'=16,'index'=8,'tensor'=2] {'index'}, dimensions={0} | all-to-all | bytes 12288 | tf_op jit(solution)/shard_map/all_to_all | solution.py:54
  81.7 7.0 gather_fusion.1
  88.7 4.9 all-to-all-start.1
  96.9 7.2 fusion.20
  104.9 5.3 mul.84
  110.2 8.2 mul.85
  118.6 116.8 %all-to-all-done.1 = bf16[8,192,2048]{2,1,0:T(8,128)(2,1)} async-done(((bf16[8,192,2048]{2,1,0:T(8,128)(2,1)}), bf16[8,192,2048]{2,1,0:T(8,128)(2,1)}, u32[]{:S(2)}, u32[]{:S(2)}) %all-to-all-start.1) | async-done | bytes 6291488 | tf_op jit(solution)/shard_map/all_to_all | solution.py:57
  235.4 23.2 %gather_fusion.2 = bf16[896,2048]{1,0:T(8,128)(2,1)} fusion(bf16[8,192,2048]{2,1,0:T(8,128)(2,1)} %all-to-all-done.1, s32[896]{0:T(1024)S(1)} %get-tuple-element.5), kind=kCustom, calls=%fused_computation.2 | custom fusion | bytes 7347200 | tf_op jit(solution)/shard_map/gather | solution.py:60
  258.6 6.0 reshape.168
  264.6 4.9 fusion.6
  277.0 6.8 all-to-all-start.2
  284.1 5.3 multiply_convert_fusion
  289.4 3.4 broadcast_in_dim.8
  292.9 162.5 %scatter_fusion.1 = bf16[8,192,2048]{2,1,0:T(8,128)(2,1)} fusion(bf16[8,192,2048]{2,1,0:T(8,128)(2,1)} %broadcast_in_dim.8, s32[896]{0:T(1024)S(1)} %get-tuple-element.6, bf16[896,2048]{1,0:T(8,128)(2,1)} %multiply_convert_fusion), kind=kCustom, calls=%fused_computation.5 | custom fusion | bytes 11017216 | tf_op jit(solution)/shard_map/scatter | solution.py:88
  455.4 4.7 all-to-all-start.3
  460.3 421.4 %psum.53 = f32[]{:T(128)} all-reduce(f32[]{:T(128)} %get-tuple-element.11), channel_id=1, replica_groups=mesh['group'=16,'index'=8,'tensor'=2] {'group','index'}, use_global_device_ids=true, to_apply=%region_14.15 | all-reduce | flops 1 | bytes 8 | tf_op jit(solution)/shard_map/psum | solution.py:68
  885.9 6.3 multiply_reduce_fusion.1
  892.2 4.7 fusion.22
  896.9 4.3 scatter_custom_fusion.1
  901.2 25.3 %scatter_custom_fusion.3 = f32[512,2048]{1,0:T(8,128)} fusion(f32[512,2048]{1,0:T(8,128)} %scatter_custom_fusion.1, s32[1536]{0:T(1024)S(1)} %fusion.11, bf16[1536,2048]{1,0:T(8,128)(2,1)} %bitcast.15), kind=kCustom, calls=%fused_computation.7 | custom fusion | flops 6291456 | bytes 10485760 | tf_op jit(solution)/shard_map/scatter-add | solution.py:91
  929.4 58.1 %all-reduce = (f32[128]{0:T(128)S(1)}, f32[512]{0:T(512)S(1)}) all-reduce(f32[128]{0:T(128)S(1)} %get-tuple-element.15, f32[512]{0:T(512)S(1)} %multiply_reduce_fusion), channel_id=1, replica_groups=mesh['group'=16,'index'=8,'tensor'=2] {'tensor'}, use_global_device_ids=true, to_apply=%region_16.17 | all-reduce | flops 640 | bytes 5120 | tf_op jit(solution)/shard_map/psum | solution.py:94
  987.5 4.4 divide_convert_fusion
  (74 shorter events, 30.8 us)
Async XLA Ops:
  7.2 11.1 %copy-start.7 = (s32[128]{0:T(128)S(1)}, s32[128]{0:T(128)}, u32[]{:S(2)}) copy-start(s32[128]{0:T(128)} %param.7) | copy-start | bytes 1540
  7.2 89.7 %all-gather.6.cloned.1.call-start = ((), (), s32[]{:S(2)}) async-start(), calls=%async_computation.6 | async-start | bytes 8912896 | tf_op jit(solution)/shard_map/all_gather | solution.py:45
  15.9 4.2 copy-start.6
  15.9 7.4 copy-start.5
  88.7 5.0 copy-start.2
  88.7 146.7 %all-to-all-start.1 = ((bf16[8,192,2048]{2,1,0:T(8,128)(2,1)}), bf16[8,192,2048]{2,1,0:T(8,128)(2,1)}, u32[]{:S(2)}, u32[]{:S(2)}) async-start(bf16[8,192,2048]{2,1,0:T(8,128)(2,1)} %bitcast.39), calls=%async_computation.1 | async-start | bytes 12582912 | tf_op jit(solution)/shard_map/all_to_all | solution.py:57
  93.7 178.6 %all-reduce.4.cloned.1.call-start = ((), (), s32[]{:S(2)}) async-start(), calls=%async_computation.4 | async-start | bytes 2097152 | tf_op jit(solution)/shard_map/psum | solution.py:66
  93.9 10.2 %copy-start.1 = (bf16[128,2048]{1,0:T(8,128)(2,1)}, bf16[128,2048]{1,0:T(8,128)(2,1)S(1)}, u32[]{:S(2)}) copy-start(bf16[128,2048]{1,0:T(8,128)(2,1)S(1)} %fusion.17) | copy-start | bytes 1572868
  104.2 788.1 %all-gather.4.cloned.1.call-start = ((), (), s32[]{:S(2)}) async-start(), calls=%async_computation.5 | async-start | bytes 8912896 | tf_op jit(solution)/shard_map/all_gather | solution.py:77
  277.0 178.4 %all-to-all-start.2 = ((bf16[128,16,128]{2,0,1:T(8,128)(2,1)}), bf16[128,16,128]{2,0,1:T(8,128)(2,1)S(1)}, u32[]{:S(2)}, u32[]{:S(2)}) async-start(bf16[128,16,128]{2,0,1:T(8,128)(2,1)} %copy_bitcast_fusion), calls=%async_computation.2 | async-start | bytes 1048576 | tf_op jit(solution)/shard_map/all_to_all | solution.py:74
  455.4 445.8 %all-to-all-start.3 = ((bf16[8,192,2048]{2,1,0:T(8,128)(2,1)}), bf16[8,192,2048]{2,1,0:T(8,128)(2,1)}, u32[]{:S(2)}, u32[]{:S(2)}) async-start(bf16[8,192,2048]{2,1,0:T(8,128)(2,1)} %scatter_fusion.1), calls=%async_computation.3 | async-start | bytes 12582912 | tf_op jit(solution)/shard_map/all_to_all | solution.py:90
  460.1 425.8 %copy-start.3 = (f32[128,2048]{1,0:T(8,128)S(1)}, f32[128,2048]{1,0:T(8,128)}, u32[]{:S(2)}) copy-start(f32[128,2048]{1,0:T(8,128)} %all-reduce.4.cloned.1.call-done) | copy-start | bytes 3145732
  901.2 25.3 %copy-start = (bf16[512,2048]{1,0:T(8,128)(2,1)S(1)}, bf16[512,2048]{1,0:T(8,128)(2,1)}, u32[]{:S(2)}) copy-start(bf16[512,2048]{1,0:T(8,128)(2,1)} %param.6) | copy-start | bytes 6291460
  987.5 4.4 copy-start.4
Sparse Core Ops, SparseCore 0:
  20.2 76.6 all-gather.5
  104.3 30.9 all-reduce.3
  138.0 76.3 all-gather.3
where the time goes:
time: 1010 us; the launch traced here: 1000 us
  blocking collectives  500 us (50%)
  local copies, waits for them, and re-layouts  265 us (26%)
  waiting for transfers between devices  120 us (12%)
  other arithmetic  56.4 us (6%)
  matrix products  26.5 us (3%)
  starting transfers between devices  16.7 us (2%)
  between operations  15.8 us (2%)
    psum x1, blocking collectives, on_device(): summed_loss = lax.psum(loss_part, ('group', 'index'))  421 us
    scatter x1, local copies, waits for them, and re-layouts, on_device(): outgoing = jnp.zeros((owners, capacity, width), jnp.bfloat16).at[owner_id...  163 us
    all_to_all x1, waiting for transfers between devices, on_device(): lax.all_to_all(fetched, 'index', split_axis=0, concat_axis=0, tiled=True)  117 us
    psum x1, blocking collectives, on_device(): lax.psum((jnp.sum(unit_query * query_hat_grad, axis=1), jnp.sum(unit_pass...  58.1 us
    scatter x1, local copies, waits for them, and re-layouts, on_device(): jnp.zeros((owners, capacity), jnp.int32).at[owner_ids, position]  45 us
    scatter-add x1, other arithmetic, on_device(): passage_hat_grad.at[asked_slots.reshape(-1)]  25.3 us
    gather x1, local copies, waits for them, and re-layouts, on_device(): hard_rows = answered[owner_ids, position].reshape(q_rows, negatives, width)  23.2 us
  transfers between devices with their start and end apart: 6, of which 2 were waited for; matrix products, arithmetic and copies ran while one was open for 31% of the time, Pallas kernels for 0%

commit v1 on v0

v1 whole, which is shorter than its diff:
```python
import jax
import jax.numpy as jnp
from jax import lax
from jax.experimental import pallas as pl
from jax.experimental.pallas import tpu as pltpu
from jax.sharding import PartitionSpec as P

epsilon = 1e-06
inverse_temp = 50.0
side = 4
lanes = 128
f32 = jnp.float32
bf16 = jnp.bfloat16


def dot_nt(a, b):
    return lax.dot_general(a, b, (((1,), (1,)), ((), ())), preferred_element_type=f32)


def dot_nn(a, b):
    return jnp.dot(a, b, preferred_element_type=f32)


def tile_lanes(values, count):
    return jnp.concatenate([values] * count, axis=1)


def fold_lanes(values):
    total = values[:, :lanes]
    for k in range(1, values.shape[1] // lanes):
        total = total + values[:, k * lanes : (k + 1) * lanes]
    return total


def to_column(row):
    return jnp.transpose(jnp.broadcast_to(row, (lanes, lanes)))


def kernel(
    slot_ref,
    offset_ref,
    hard_slot_ref,
    q_hbm,
    p_hbm,
    loss_ref,
    dq_ref,
    dp_ref,
    p_ref,
    zq,
    sh_mine,
    sh_peer,
    eh_t,
    eh,
    zs_send,
    zs_recv,
    pq,
    xq,
    yp,
    si_mine,
    si_peer,
    ein_t,
    ein_s,
    ein,
    pin,
    xs_send,
    xs_recv,
    ys_send,
    ys_recv,
    dq_acc,
    dp_acc,
    wt,
    pick,
    norm_mine,
    norm_peer,
    pcol,
    qcol,
    aux_own,
    aux_z,
    aux_x,
    pos_own,
    aux_y,
    sum_out,
    sum_z,
    sum_x,
    fac_own,
    fac_z,
    fac_x,
    own_out,
    own_y,
    loss_z,
    loss_x,
    loss_y,
    along_p_mine,
    along_p_peer,
    own_col,
    rest_col,
    ratio_col,
    along_col,
    send_sems,
    recv_sems,
    load_sems,
):
    rows, width = q_hbm.shape
    p_rows = p_ref.shape[0]
    half = rows // 2
    tiles = p_rows // rows
    group = lax.axis_index("group")
    z = lax.axis_index("index")
    t = lax.axis_index("tensor")
    y = lax.div(group, side)
    x = lax.rem(group, side)
    owners = lax.axis_size("index")

    def at_z(k):
        return (group, lax.rem(z + k + owners, owners), t)

    def at_x(k):
        return (y * side + lax.rem(x + k + side, side), z, t)

    def at_y(k):
        return (lax.rem(y + k + side, side) * side + x, z, t)

    other = (group, z, 1 - t)

    sent = []
    done = [0]

    def drain(count):
        for copy in sent[done[0] : count]:
            copy.wait_send()
        done[0] = max(done[0], count)

    def send(src, dst, target):
        k = len(sent)
        copy = pltpu.make_async_remote_copy(
            src_ref=src,
            dst_ref=dst,
            send_sem=send_sems.at[k],
            recv_sem=recv_sems.at[k],
            device_id=target,
            device_id_type=pl.DeviceIdType.MESH,
        )
        copy.start()
        sent.append(copy)
        return copy

    def rows_of(slot, part=None):
        if part is None:
            return pl.ds(slot * rows, rows)
        return pl.ds(slot * rows + part * half, half)

    far = 6

    def place(k, before, start):
        if k == 4:
            return far * rows + start
        return (2 * (k - 1) + int((start < half) != before)) * rows + start

    first_lanes = lax.broadcasted_iota(jnp.int32, (1, lanes), 1) < half

    def of_tile(tile, pair):
        if tile == far:
            return pair(far)
        block = tile - tile % 2
        low, high = (block, block + 1) if tile == block else (block + 1, block)
        return jnp.where(first_lanes, pair(low), pair(high))

    z_targets = [at_z(1), at_z(-1), at_z(2), at_z(-2), at_z(3), at_z(-3), at_z(4)]
    z_homes = [at_z(-1), at_z(1), at_z(-2), at_z(2), at_z(-3), at_z(3), at_z(4)]
    x_targets = [at_x(1), at_x(-1), at_x(2)]
    x_homes = [at_x(-1), at_x(1), at_x(2)]
    y_targets = [at_y(1), at_y(-1), at_y(2)]
    y_homes = [at_y(-1), at_y(1), at_y(2)]

    load_q = pltpu.make_async_copy(q_hbm, xq.at[rows_of(0)], load_sems.at[0])
    load_p = pltpu.make_async_copy(p_hbm, p_ref, load_sems.at[1])
    load_q.start()
    load_p.start()

    barrier = pltpu.get_barrier_semaphore()
    peers = z_targets + x_targets + y_targets + [other]
    for peer in peers:
        pl.semaphore_signal(barrier, inc=1, device_id=peer, device_id_type=pl.DeviceIdType.MESH)
    pl.semaphore_wait(barrier, len(peers))

    def z_rows(k, before, c):
        return pl.ds(place(k, before, c * half), half)

    z_right = {}
    z_left = {}
    for c in range(2):
        right_own = q_hbm.at[pl.ds(c * half, half)]
        left_own = q_hbm.at[pl.ds((1 - c) * half, half)]
        z_right[1, c] = send(right_own, zq.at[z_rows(1, True, c)], at_z(1))
        z_left[1, 1 - c] = send(left_own, zq.at[z_rows(1, False, 1 - c)], at_z(-1))
    x_right = send(q_hbm, xq.at[rows_of(1)], at_x(1))
    x_left = send(q_hbm, xq.at[rows_of(2)], at_x(-1))
    load_q.wait()
    load_p.wait()
    q_ref = xq

    slots = slot_ref[0:1, :]
    for i in range(tiles):
        ids = lax.broadcasted_iota(jnp.int32, (rows, lanes), 0) + i * rows
        chosen = jnp.where(ids == slots, 1.0, 0.0).astype(f32)
        pick[:, i * rows : (i + 1) * rows] = jnp.transpose(chosen).astype(bf16)
        wt[i * rows : (i + 1) * rows, 7 * rows : 8 * rows] = chosen.astype(bf16)
        wt[i * rows : (i + 1) * rows, 8 * rows : 9 * rows] = chosen.astype(bf16)

    wide = 512

    def pick_columns(i, _):
        columns = pl.ds(pl.multiple_of(i * wide, wide), wide)
        yp[0:rows, columns] = dot_nn(pick[...], p_ref[:, columns]).astype(bf16)
        return 0

    lax.fori_loop(0, width // wide, pick_columns, 0)
    y_right = send(yp.at[rows_of(0)], yp.at[rows_of(1)], at_y(1))
    y_left = send(yp.at[rows_of(0)], yp.at[rows_of(2)], at_y(-1))

    strip = 32

    def square_strip(source, base):
        def body(i, _):
            part = pl.ds(pl.multiple_of(i * strip, strip), strip)
            values = source[part, :].astype(f32)
            norm_mine[pl.ds(pl.multiple_of(base + i * strip, strip), strip), :] = fold_lanes(
                values * values
            )
            return 0

        return body

    lax.fori_loop(0, p_rows // strip, square_strip(p_ref, 0), 0)
    lax.fori_loop(0, rows // strip, square_strip(q_ref, p_rows), 0)
    norm_copy = send(norm_mine, norm_peer, other)
    norm_copy.wait_recv()

    def scale_of(start):
        squares = norm_mine[start : start + rows, :] + norm_peer[start : start + rows, :]
        total = jnp.sum(squares, axis=1, keepdims=True)
        return jnp.broadcast_to(1.0 / jnp.sqrt(total + epsilon), (rows, lanes))

    position_row = jnp.zeros((1, lanes), f32)
    for i in range(tiles):
        scale = scale_of(i * rows)
        pcol[i * rows : (i + 1) * rows, :] = scale
        ids = lax.broadcasted_iota(jnp.int32, (rows, lanes), 0) + i * rows
        position_row = position_row + jnp.sum(
            jnp.where(ids == slots, scale, 0.0), axis=0, keepdims=True
        )
    q_scale = scale_of(p_rows)
    qcol[...] = q_scale
    q_row = jnp.transpose(q_scale)[0:1, :]
    owner_ids = lax.rem(offset_ref[...] + (z + 1), owners)
    aux_own[0:7, :] = (owner_ids * p_rows + hard_slot_ref[...]).astype(f32)
    aux_own[7:8, :] = q_row
    pos_own[...] = jnp.broadcast_to(position_row, (8, lanes))
    aux_z_copies = [send(aux_own, aux_z.at[m], z_targets[m]) for m in range(7)]
    aux_x_copies = [send(aux_own, aux_x.at[m], x_targets[m]) for m in range(3)]
    aux_y_copies = [send(pos_own, aux_y.at[m], y_targets[m]) for m in range(3)]

    def forward_z(k, c):
        z_right[k, c].wait_recv()
        here = zq.at[z_rows(k, True, c)]
        if k < 3 or c == 0:
            z_right[k + 1, c] = send(here, zq.at[z_rows(k + 1, True, c)], at_z(1))
        z_left[k, 1 - c].wait_recv()
        here = zq.at[z_rows(k, False, 1 - c)]
        if k < 3 or c == 0:
            z_left[k + 1, 1 - c] = send(here, zq.at[z_rows(k + 1, False, 1 - c)], at_z(-1))

    line = lax.broadcasted_iota(jnp.int32, (8, lanes), 0)
    hard_copies = {}

    def hard_part(tile, count):
        def body(i, _):
            part = pl.ds(pl.multiple_of(i * 256, 256), 256)
            scores = dot_nt(p_ref[part, :], zq[tile * rows : (tile + count) * rows, :])
            for n in range(count):
                sh_mine[tile + n, part, :] = scores[:, n * lanes : (n + 1) * lanes]
            return 0

        lax.fori_loop(0, p_rows // 256, body, 0)
        here = pl.ds(tile, count)
        copy = send(sh_mine.at[here], sh_peer.at[here], other)
        for n in range(count):
            hard_copies[tile + n] = copy if n == 0 else None

    first_slot = (z * p_rows).astype(f32)
    hard_sums = {}

    def hard_exp(tile):
        if hard_copies[tile] is not None:
            hard_copies[tile].wait_recv()
        if tile == far or tile % 2 == 0:
            for block in (far,) if tile == far else (tile, tile + 1):
                aux_z_copies[block].wait_recv()
        packet = of_tile(tile, lambda block: aux_z[block])
        row_scale = inverse_temp * packet[7:8, :]
        columns = slice(tile * rows, (tile + 1) * rows)

        def body(i, carry):
            sums, moments = carry
            part = pl.ds(pl.multiple_of(i * rows, rows), rows)
            ids = (
                lax.broadcasted_iota(jnp.int32, (rows, lanes), 0) + i * rows
            ).astype(f32) + first_slot
            times = jnp.zeros((rows, lanes), f32)
            for j in range(7):
                times = times + jnp.where(ids == packet[j : j + 1, :], 1.0, 0.0)
            scale = pcol[part, :]
            score = (sh_mine[tile, part, :] + sh_peer[tile, part, :]) * (scale * row_scale)
            weight = jnp.where(times > 0.0, times * jnp.exp(score), 0.0)
            eh_t[part, columns] = weight
            eh[columns, part] = jnp.transpose(weight * scale).astype(bf16)
            return (
                sums + jnp.sum(weight, axis=0, keepdims=True),
                moments + jnp.sum(weight * score, axis=0, keepdims=True),
            )

        zero = jnp.zeros((1, lanes), f32)
        sums, moments = lax.fori_loop(0, tiles, body, (zero, zero))
        hard_sums[tile] = jnp.where(line == 0, sums, moments)

    sum_z_copies = {}

    def send_hard_sum(slot):
        sum_out[slot] = of_tile(slot, lambda tile: hard_sums[tile])
        sum_z_copies[slot] = send(sum_out.at[slot], sum_z.at[slot], z_homes[slot])

    def in_product(start, stop, other_rows):
        def body(i, _):
            columns = pl.ds(pl.multiple_of(i * wide, wide), wide)
            pin[start:stop, columns] = dot_nn(ein[start:stop, :], other_rows[:, columns])
            return 0

        lax.fori_loop(0, width // wide, body, 0)

    grain = 16

    def stage(dst, dst_row, src, src_row, count, add=None, add_row=0):
        def body(i, _):
            values = src[pl.ds(pl.multiple_of(src_row + i * grain, grain), grain), :]
            if add is not None:
                values = values + add[
                    pl.ds(pl.multiple_of(add_row + i * grain, grain), grain), :
                ].astype(f32)
            dst[pl.ds(pl.multiple_of(dst_row + i * grain, grain), grain), :] = values.astype(
                dst.dtype
            )
            return 0

        lax.fori_loop(0, count // grain, body, 0)

    def square_first(send_buffer, recv_buffer, at):
        stage(send_buffer, 2 * rows, pin, 3 * rows, rows)
        return (
            send(send_buffer.at[rows_of(2, 0)], recv_buffer.at[rows_of(2, 0)], at(1)),
            send(send_buffer.at[rows_of(2, 1)], recv_buffer.at[rows_of(2, 1)], at(-1)),
        )

    def square_free(send_buffer, recv_buffer, at):
        stage(send_buffer, 0, pin, rows, half)
        before = send(send_buffer.at[rows_of(0, 0)], recv_buffer.at[rows_of(0, 0)], at(-1))
        stage(send_buffer, rows + half, pin, 2 * rows + half, half)
        after = send(send_buffer.at[rows_of(1, 1)], recv_buffer.at[rows_of(1, 1)], at(1))
        return [before, after]

    def square_last(first, send_buffer, recv_buffer, at):
        first[0].wait_recv()
        stage(send_buffer, rows, pin, 2 * rows, half, recv_buffer, 2 * rows)
        after = send(send_buffer.at[rows_of(1, 0)], recv_buffer.at[rows_of(1, 0)], at(1))
        first[1].wait_recv()
        stage(send_buffer, half, pin, rows + half, half, recv_buffer, 2 * rows + half)
        before = send(send_buffer.at[rows_of(0, 1)], recv_buffer.at[rows_of(0, 1)], at(-1))
        return [before, after]

    in_sums = [jnp.zeros((1, lanes), f32) for _ in range(side)]
    in_moments = [jnp.zeros((1, lanes), f32) for _ in range(side)]
    diagonal = lax.broadcasted_iota(jnp.int32, (rows, lanes), 0) == lax.broadcasted_iota(
        jnp.int32, (rows, lanes), 1
    )

    def in_part(c_start, c_stop, n_start, n_stop):
        def body(i, _):
            part = pl.ds(pl.multiple_of(c_start * rows + i * rows, rows), rows)
            scores = dot_nt(yp[part, :], xq[n_start * rows : n_stop * rows, :])
            for n in range(n_start, n_stop):
                k = (n - n_start) * lanes
                si_mine[n, part, :] = scores[:, k : k + lanes]
            return 0

        lax.fori_loop(0, c_stop - c_start, body, 0)
        block = (pl.ds(n_start, n_stop - n_start), pl.ds(c_start * rows, (c_stop - c_start) * rows))
        return send(si_mine.at[block], si_peer.at[block], other)

    def in_exp(c, n):
        c_row = position_row if c == 0 else aux_y[c - 1][0:1, :]
        scale = to_column(c_row)
        part = slice(c * rows, (c + 1) * rows)
        row_scale = inverse_temp * (q_row if n == 0 else aux_x[n - 1][7:8, :])
        columns = slice(n * rows, (n + 1) * rows)
        score = (si_mine[n, part, :] + si_peer[n, part, :]) * (scale * row_scale)
        weight = jnp.exp(score)
        own = None
        if c == 0 and n == 0:
            own = jnp.sum(jnp.where(diagonal, score, 0.0), axis=0, keepdims=True)
            weight = jnp.where(diagonal, 0.0, weight)
        ein_t[part, columns] = weight
        ein_s[part, columns] = weight * score
        ein[columns, part] = jnp.transpose(weight * scale).astype(bf16)
        in_sums[n] = in_sums[n] + jnp.sum(weight, axis=0, keepdims=True)
        in_moments[n] = in_moments[n] + jnp.sum(weight * score, axis=0, keepdims=True)
        return own

    forward_z(1, 0)
    hard_part(0, 1)
    hard_exp(0)
    forward_z(1, 1)
    x_right.wait_recv()
    x_far_right = send(xq.at[rows_of(1, 0)], xq.at[rows_of(3, 0)], at_x(1))
    x_left.wait_recv()
    x_far_left = send(xq.at[rows_of(2, 1)], xq.at[rows_of(3, 1)], at_x(-1))
    y_right.wait_recv()
    y_far_right = send(yp.at[rows_of(1, 0)], yp.at[rows_of(3, 0)], at_y(1))
    y_left.wait_recv()
    y_far_left = send(yp.at[rows_of(2, 1)], yp.at[rows_of(3, 1)], at_y(-1))
    hard_part(1, 1)
    near_copy = in_part(0, 3, 0, 3)
    hard_exp(1)
    for copy in aux_x_copies + aux_y_copies:
        copy.wait_recv()
    near_copy.wait_recv()
    own_score = in_exp(0, 0)
    for c in range(3):
        for n in range(3):
            if c or n:
                in_exp(c, n)
    forward_z(2, 0)
    hard_part(2, 1)
    x_far_right.wait_recv()
    x_far_left.wait_recv()
    far_x_copy = in_part(0, 3, 3, 4)
    y_far_right.wait_recv()
    y_far_left.wait_recv()
    far_y_copy = in_part(3, 4, 0, 4)
    hard_exp(2)
    far_x_copy.wait_recv()
    for c in range(3):
        in_exp(c, 3)
    far_y_copy.wait_recv()
    for n in range(side):
        in_exp(3, n)
    sum_x_copies = []
    for n in range(1, side):
        sum_out[6 + n] = jnp.where(line == 0, in_sums[n], in_moments[n])
        sum_x_copies.append(send(sum_out.at[6 + n], sum_x.at[n - 1], x_homes[n - 1]))
    in_product(3 * rows, 4 * rows, yp)
    x_first = square_first(xs_send, xs_recv, at_x)
    forward_z(2, 1)
    hard_part(3, 1)
    in_product(0, 3 * rows, yp)
    x_second = square_free(xs_send, xs_recv, at_x)
    hard_exp(3)
    forward_z(3, 0)
    hard_part(4, 1)
    x_second += square_last(x_first, xs_send, xs_recv, at_x)
    hard_exp(4)

    def hard_query(slot, count, base):
        def body(i, _):
            columns = pl.ds(pl.multiple_of(i * wide, wide), wide)
            pq[base : base + count * rows, columns] = dot_nn(
                eh[slot * rows : (slot + count) * rows, :], p_ref[:, columns]
            )
            return 0

        lax.fori_loop(0, width // wide, body, 0)

    back_right = {}
    back_left = {}

    pq_base = {3: 0, 2: 2 * rows, 1: 0, 4: 4 * rows}

    def stage_back(k, start, count, right, came=None, wait=True):
        first = place(k, not right, start)
        base = first - 2 * (k - 1) * rows + pq_base[k]
        if came is None:
            stage(zs_send, first, pq, base, count)
        else:
            if wait:
                (back_right if right else back_left)[came].wait_recv()
            stage(zs_send, first, pq, base, count, zs_recv, place(k + 1, not right, start))

    def start_back(k, start, count, right):
        here = pl.ds(place(k, not right, start), count)
        (back_right if right else back_left)[k, start] = send(
            zs_send.at[here], zs_recv.at[here], at_z(1 if right else -1)
        )

    def send_back(k, start, count, right, came=None, wait=True):
        stage_back(k, start, count, right, came, wait)
        start_back(k, start, count, right)

    hard_query(4, 1, 0)
    stage_back(3, half, half, True)
    stage_back(3, 0, half, False)
    forward_z(3, 1)
    hard_part(5, 1)
    start_back(3, half, half, True)
    start_back(3, 0, half, False)
    hard_exp(5)
    for slot in range(6):
        send_hard_sum(slot)
    z_right[4, 0].wait_recv()
    z_left[4, 1].wait_recv()
    hard_part(far, 1)
    hard_query(5, 1, rows)
    hard_exp(far)
    send_hard_sum(far)
    hard_query(far, 1, 4 * rows)
    send_back(4, 0, half, True)
    send_back(4, half, half, False)
    older = len(sent) - 8

    rest = in_sums[0]
    moment = in_moments[0]
    for m in range(3):
        sum_x_copies[m].wait_recv()
        rest = rest + sum_x[m][0:1, :]
        moment = moment + sum_x[m][1:2, :]
    for m in range(7):
        sum_z_copies[m].wait_recv()
        rest = rest + sum_z[m][0:1, :]
        moment = moment + sum_z[m][1:2, :]
    total = rest + jnp.exp(own_score)
    ratio = inverse_temp / total
    factor = ratio * q_row
    inverse = 1.0 / total
    fac_own[...] = jnp.where(line == 0, factor, inverse)
    fac_x_copies = [send(fac_own, fac_x.at[m], x_targets[m]) for m in range(3)]
    fac_z_copies = [send(fac_own, fac_z.at[m], z_targets[m]) for m in range(7)]
    loss_z[z] = jnp.broadcast_to(jnp.log(total) - own_score, (8, lanes))
    loss_z_copies = [send(loss_z.at[z], loss_z.at[z], at_z(k)) for k in range(1, 8)]

    hard_query(2, 2, 2 * rows)

    along = (moment - rest * own_score) / total
    own_col[...] = to_column(factor * rest)
    ratio_col[...] = to_column(factor)
    rest_col[...] = to_column(factor * rest * position_row)
    along_col[...] = to_column(along * q_row * q_row)
    repeat = width // lanes

    for copy in fac_x_copies:
        copy.wait_recv()
    for n in range(side):
        fac_row = factor if n == 0 else fac_x[n - 1][0:1, :]
        columns = slice(n * rows, (n + 1) * rows)
        for c in range(side):
            part = slice(c * rows, (c + 1) * rows)
            ein[part, columns] = (ein_t[part, columns] * fac_row).astype(bf16)

    in_product(3 * rows, 4 * rows, xq)
    y_first = square_first(ys_send, ys_recv, at_y)
    send_back(2, half, half, True, came=(3, half))
    send_back(2, 0, half, False, came=(3, 0))
    in_product(rows, 3 * rows, xq)
    y_second = square_free(ys_send, ys_recv, at_y)

    for copy in x_second:
        copy.wait_recv()

    def gather_x(i, _):
        part = pl.ds(pl.multiple_of(i * grain, grain), grain)
        after = pl.ds(pl.multiple_of(rows + i * grain, grain), grain)
        values = pin[part, :] + (
            xs_recv[part, :].astype(f32) + xs_recv[after, :].astype(f32)
        )
        dq_acc[part, :] = (
            values * tile_lanes(ratio_col[part, :], repeat)
            - yp[part, :].astype(f32) * tile_lanes(rest_col[part, :], repeat)
            - q_ref[part, :].astype(f32) * tile_lanes(along_col[part, :], repeat)
        )
        return 0

    lax.fori_loop(0, rows // grain, gather_x, 0)

    in_product(0, rows, xq)

    own_along = None
    own_copies = []
    for c in range(side):
        part = slice(c * rows, (c + 1) * rows)
        shares = jnp.zeros((rows, lanes), f32)
        for n in range(side):
            inverse_row = inverse if n == 0 else fac_x[n - 1][1:2, :]
            shares = shares + ein_s[part, n * rows : (n + 1) * rows] * inverse_row
        row = jnp.sum(jnp.transpose(shares), axis=0, keepdims=True)
        if c == 0:
            own_along = row - rest * own_score * inverse
        else:
            own_out[c - 1] = jnp.broadcast_to(row, (8, lanes))
            own_copies.append(send(own_out.at[c - 1], own_y.at[c - 1], y_homes[c - 1]))
    send_back(3, 0, half, True, came=(4, 0))
    send_back(3, half, half, False, came=(4, half))
    hard_query(0, 2, 0)

    for m in range(7):
        fac_z_copies[m].wait_recv()
    for m in range(7):
        columns = slice(m * rows, (m + 1) * rows)
        fac_row = of_tile(m, lambda block: fac_z[block][0:1, :])
        for c in range(tiles):
            part = slice(c * rows, (c + 1) * rows)
            wt[part, columns] = (eh_t[part, columns] * fac_row).astype(bf16)

    y_second += square_last(y_first, ys_send, ys_recv, at_y)
    send_back(1, half, half, True, came=(2, half))
    send_back(1, 0, half, False, came=(2, 0))

    def passage_hard(i, _):
        columns = pl.ds(pl.multiple_of(i * 256, 256), 256)
        dp_acc[:, columns] = dot_nn(wt[:, 0 : 7 * rows], zq[0 : 7 * rows, columns])
        return 0

    lax.fori_loop(0, width // 256, passage_hard, 0)
    drain(older)

    def passage_along(i, _):
        part = pl.ds(pl.multiple_of(i * grain, grain), grain)
        along_p_mine[part, :] = fold_lanes(dp_acc[part, :] * p_ref[part, :].astype(f32))
        return 0

    lax.fori_loop(0, p_rows // grain, passage_along, 0)
    along_p_copy = send(along_p_mine, along_p_peer, other)
    quarter = half // 2
    for start in (0, quarter):
        send_back(2, start, quarter, True, came=(3, 0), wait=start == 0)
        send_back(2, half + start, quarter, False, came=(3, half), wait=start == 0)

    for copy in loss_z_copies:
        copy.wait_recv()
    value = loss_z[0]
    for k in range(1, 8):
        value = value + loss_z[k]
    loss_x[x] = value
    loss_x_copies = [send(loss_x.at[x], loss_x.at[x], at_x(k)) for k in range(1, side)]
    older = len(sent) - 8
    for copy in loss_x_copies:
        copy.wait_recv()
    value = loss_x[0]
    for k in range(1, side):
        value = value + loss_x[k]
    loss_y[y] = value
    loss_y_copies = [send(loss_y.at[y], loss_y.at[y], at_y(k)) for k in range(1, side)]

    for m in range(3):
        own_copies[m].wait_recv()
        own_along = own_along + own_y[m][0:1, :]
    along_p_copy.wait_recv()
    for copy in y_second:
        copy.wait_recv()

    def positive_rows(i, _):
        part = pl.ds(pl.multiple_of(i * grain, grain), grain)
        after = pl.ds(pl.multiple_of(rows + i * grain, grain), grain)
        values = pin[part, :] + (ys_recv[part, :].astype(f32) + ys_recv[after, :].astype(f32))
        values = values - tile_lanes(own_col[part, :], repeat) * q_ref[part, :].astype(f32)
        high = values.astype(bf16)
        zq[pl.ds(pl.multiple_of(7 * rows + i * grain, grain), grain), :] = high
        zq[pl.ds(pl.multiple_of(8 * rows + i * grain, grain), grain), :] = (
            values - high.astype(f32)
        ).astype(bf16)
        return 0

    lax.fori_loop(0, rows // grain, positive_rows, 0)

    def passage_out(i, _):
        part = pl.ds(pl.multiple_of(i * rows, rows), rows)
        scale = pcol[part, :]
        shares = (along_p_mine[part, :] + along_p_peer[part, :]) * scale
        shares = shares + wt[part, 7 * rows : 8 * rows].astype(f32) * own_along
        along = jnp.sum(shares, axis=1, keepdims=True)
        along = jnp.broadcast_to(along, (rows, lanes)) * scale
        for c in range(width // wide):
            columns = slice(c * wide, (c + 1) * wide)
            values = dp_acc[part, columns] + dot_nn(
                wt[part, 7 * rows : 9 * rows], zq[7 * rows : 9 * rows, columns]
            )
            dp_ref[part, columns] = (
                (values - p_ref[part, columns].astype(f32) * tile_lanes(along, wide // lanes))
                * tile_lanes(scale, wide // lanes)
            ).astype(bf16)
        return 0

    lax.fori_loop(0, tiles // 2, passage_out, 0)
    send_back(1, 0, quarter, True, came=(2, 0))
    send_back(1, half, quarter, False, came=(2, half))
    lax.fori_loop(tiles // 2, tiles, passage_out, 0)
    send_back(1, quarter, quarter, True, came=(2, quarter))
    send_back(1, half + quarter, quarter, False, came=(2, half + quarter))
    for copy in loss_y_copies:
        copy.wait_recv()
    value = loss_y[0]
    for k in range(1, side):
        value = value + loss_y[k]
    queries = rows * owners * side * side
    loss_ref[0, 0] = jnp.sum(value[0:1, :]) * (1.0 / queries)
    drain(older)

    def query_out(first):
        def body(i, _):
            part = pl.ds(pl.multiple_of(first + i * grain, grain), grain)
            before = pl.ds(pl.multiple_of(place(1, True, first) + i * grain, grain), grain)
            after = pl.ds(pl.multiple_of(place(1, False, first) + i * grain, grain), grain)
            back = zs_recv[before, :].astype(f32) + zs_recv[after, :].astype(f32)
            dq_ref[part, :] = (
                dq_acc[part, :] + back * tile_lanes(ratio_col[part, :], repeat)
            ).astype(bf16)
            return 0

        lax.fori_loop(0, quarter // grain, body, 0)

    back_right[1, half].wait_recv()
    back_left[1, 0].wait_recv()
    for start in (0, quarter):
        back_right[1, start].wait_recv()
        query_out(start)
        back_left[1, half + start].wait_recv()
        query_out(half + start)
    drain(len(sent))


def flush(dq_ref, dp_ref, dq_out, dp_out, sems):
    copies = [
        pltpu.make_async_copy(dp_ref, dp_out, sems.at[0]),
        pltpu.make_async_copy(dq_ref, dq_out, sems.at[1]),
    ]
    for copy in copies:
        copy.start()
    for copy in copies:
        copy.wait()


def on_device(queries, passages, positive_slot, hard_offset, hard_slot):
    rows, width = queries.shape
    p_rows = passages.shape[0]
    copies = 128
    vmem = pl.BlockSpec(memory_space=pltpu.VMEM)
    hbm = pl.BlockSpec(memory_space=pltpu.HBM)

    def f(*shape):
        return pltpu.VMEM(shape, f32)

    def b(*shape):
        return pltpu.VMEM(shape, bf16)

    loss, query_grad, passage_grad = pl.pallas_call(
        kernel,
        out_shape=(
            jax.ShapeDtypeStruct((1, 1), f32),
            pltpu.VMEM(queries.shape, bf16),
            pltpu.VMEM(passages.shape, bf16),
        ),
        in_specs=[vmem, vmem, vmem, hbm, hbm],
        out_specs=(pl.BlockSpec(memory_space=pltpu.SMEM), vmem, vmem),
        scratch_shapes=[
            b(p_rows, width),
            b(9 * rows, width),
            f(7, p_rows, rows),
            f(7, p_rows, rows),
            f(p_rows, 7 * rows),
            b(7 * rows, p_rows),
            b(7 * rows, width),
            b(7 * rows, width),
            f(5 * rows, width),
            b(4 * rows, width),
            b(4 * rows, width),
            f(4, 4 * rows, rows),
            f(4, 4 * rows, rows),
            f(4 * rows, 4 * rows),
            f(4 * rows, 4 * rows),
            b(4 * rows, 4 * rows),
            f(4 * rows, width),
            b(3 * rows, width),
            b(3 * rows, width),
            b(3 * rows, width),
            b(3 * rows, width),
            f(rows, width),
            f(p_rows, width),
            b(p_rows, 9 * rows),
            b(rows, p_rows),
            f(p_rows + rows, lanes),
            f(p_rows + rows, lanes),
            f(p_rows, lanes),
            f(rows, lanes),
            f(8, lanes),
            f(7, 8, lanes),
            f(3, 8, lanes),
            f(8, lanes),
            f(3, 8, lanes),
            f(10, 8, lanes),
            f(7, 8, lanes),
            f(3, 8, lanes),
            f(8, lanes),
            f(7, 8, lanes),
            f(3, 8, lanes),
            f(3, 8, lanes),
            f(3, 8, lanes),
            f(8, 8, lanes),
            f(4, 8, lanes),
            f(4, 8, lanes),
            f(p_rows, lanes),
            f(p_rows, lanes),
            f(rows, lanes),
            f(rows, lanes),
            f(rows, lanes),
            f(rows, lanes),
            pltpu.SemaphoreType.DMA((copies,)),
            pltpu.SemaphoreType.DMA((copies,)),
            pltpu.SemaphoreType.DMA((2,)),
        ],
        compiler_params=pltpu.CompilerParams(
            collective_id=0, has_side_effects=True, vmem_limit_bytes=58 * 1024 * 1024
        ),
        cost_estimate=pl.CostEstimate(
            flops=15_000_000_000, bytes_accessed=6_000_000, transcendentals=800_000
        ),
    )(positive_slot.reshape(1, rows), hard_offset.T, hard_slot.T, queries, passages)
    query_grad, passage_grad = pl.pallas_call(
        flush,
        out_shape=(
            jax.ShapeDtypeStruct(queries.shape, bf16),
            jax.ShapeDtypeStruct(passages.shape, bf16),
        ),
        in_specs=[vmem, vmem],
        out_specs=(hbm, hbm),
        scratch_shapes=[pltpu.SemaphoreType.DMA((2,))],
        compiler_params=pltpu.CompilerParams(vmem_limit_bytes=1024 * 1024),
    )(
        pltpu.with_memory_space_constraint(query_grad, pltpu.VMEM),
        pltpu.with_memory_space_constraint(passage_grad, pltpu.VMEM),
    )
    return loss[0, 0], query_grad, passage_grad


def solution(mesh):
    in_specs = (
        P(("group", "index"), "tensor"),
        P(("group", "index"), "tensor"),
        P(("group", "index")),
        P(("group", "index"), None),
        P(("group", "index"), None),
    )
    out_specs = (P(), P(("group", "index"), "tensor"), P(("group", "index"), "tensor"))
    return jax.shard_map(
        on_device, mesh=mesh, in_specs=in_specs, out_specs=out_specs, check_vma=False
    )
```

time: 1010 us -> 101 us (0.10)
  blocking collectives: 500 us -> 0 us
  local copies, waits for them, and re-layouts: 265 us -> 0 us
  waiting for transfers between devices: 120 us -> 0 us
  Pallas kernels: 0 us -> 97.8 us
  other arithmetic: 56.4 us -> 0 us
  matrix products: 26.5 us -> 0 us
  starting transfers between devices: 16.7 us -> 0 us
  between operations: 15.8 us -> 2.41 us
    psum x4 -> x0, blocking collectives: 487 us -> none  [the longest x1 421 us: on_device(): summed_loss = lax.psum(loss_part, ('group', 'index'))]
    scatter x2 -> x0, local copies, waits for them, and re-layouts: 208 us -> none  [the longest x1 163 us: on_device(): outgoing = jnp.zeros((owners, capacity, width), jnp.bfloat16).at[owner_id...]
    all_to_all x3 -> x0, waiting for transfers between devices: 117 us -> none  [the longest x1 117 us: on_device(): lax.all_to_all(fetched, 'index', split_axis=0, concat_axis=0, tiled=True)]
    pallas_call x0 -> x2, Pallas kernels: none -> 97.8 us  [the longest x1 96.3 us: on_device(): pl.pallas_call(kernel, out_shape=(jax.ShapeDtypeStruct((1, 1), f32), pltp...]
    gather x3 -> x0, local copies, waits for them, and re-layouts: 31.9 us -> none  [the longest x1 23.2 us: on_device(): hard_rows = answered[owner_ids, position].reshape(q_rows, negatives, width)]
    scatter-add x2 -> x0, other arithmetic: 29.6 us -> none  [the longest x1 25.3 us: on_device(): passage_hat_grad.at[asked_slots.reshape(-1)]]
    dot_general x5 -> x0, matrix products: 26.5 us -> none  [the longest x1 7.23 us: on_device(): lax.dot_general(query_hat, batch_block, (((1,), (1,)), ((), ())), preferr...]
    all_to_all x3 -> x0, starting transfers between devices: 16.4 us -> none  [the longest x1 6.78 us: on_device(): lax.all_to_all(weight_in, 'group', split_axis=1, concat_axis=0, tiled=True)]
  transfers between devices with their start and end apart: 6 -> 0, of which waited for: 2 -> 0; matrix products, arithmetic and copies ran while one was open for 31% -> 0% of each run, Pallas kernels for 0% -> 0%
where the time goes in v1:
time: 101 us; the launch traced here: 100 us
  Pallas kernels  97.8 us (97%)
  between operations  2.41 us (2%)
    pallas_call x1, Pallas kernels, on_device(): pl.pallas_call(kernel, out_shape=(jax.ShapeDtypeStruct((1, 1), f32), pltp...  96.3 us

profile of v1, /device:TPU:1, one launch (start us, length us, event | category | flops | bytes accessed | tf_op | source)
XLA Modules:
  0.0 100.2 jit_solution(9043544491599879558)
XLA Ops:
  0.6 96.3 %shard_map.76 = (f32[1,1]{1,0:T(1,128)}, bf16[128,2048]{1,0:T(8,128)(2,1)S(1)}, bf16[512,2048]{1,0:T(8,128)(2,1)S(1)}) custom-call(s32[1,128]{1,0:T(1,128)} %bitcast.6, s32[7,128]{1,0:T(8,128)} %bitcast.4, s32[7,128]{1,0:T(8,128)} %bitcast.5, bf16[128,2048]{1,0:T(8,128)(2,1)} %q_hbm.1, bf16[512,2048]{1,0:T(8,128)(2,1)} %p_hbm.1), custom_call_target="tpu_custom_call" | custom-call | flops 15000000512 | bytes 6000000 | tf_op jit(solution)/shard_map/pallas_call | solution.py:760
  96.9 1.5 %shard_map.77 = (bf16[128,2048]{1,0:T(8,128)(2,1)}, bf16[512,2048]{1,0:T(8,128)(2,1)}) custom-call(bf16[128,2048]{1,0:T(8,128)(2,1)S(1)} %get-tuple-element.9.dq_ref, bf16[512,2048]{1,0:T(8,128)(2,1)S(1)} %get-tuple-element.10.dp_ref), custom_call_target="tpu_custom_call" | custom-call | tf_op jit(solution)/shard_map/pallas_call | solution.py:832

commit v2 on v1

--- a/solution.py
+++ b/solution.py
@@ -74,6 +74,7 @@
     norm_peer,
     pcol,
     qcol,
+    ccol,
     aux_own,
     aux_z,
     aux_x,
@@ -329,6 +330,68 @@
         sum_out[slot] = of_tile(slot, lambda tile: hard_sums[tile])
         sum_z_copies[slot] = send(sum_out.at[slot], sum_z.at[slot], z_homes[slot])
 
+    forward_z(1, 0)
+    forward_z(1, 1)
+    x_right.wait_recv()
+    x_far_right = send(xq.at[rows_of(1, 0)], xq.at[rows_of(3, 0)], at_x(1))
+    x_left.wait_recv()
+    x_far_left = send(xq.at[rows_of(2, 1)], xq.at[rows_of(3, 1)], at_x(-1))
+    y_right.wait_recv()
+    y_far_right = send(yp.at[rows_of(1, 0)], yp.at[rows_of(3, 0)], at_y(1))
+    y_left.wait_recv()
+    y_far_left = send(yp.at[rows_of(2, 1)], yp.at[rows_of(3, 1)], at_y(-1))
+    hard_part(0, 2)
+    hard_exp(0)
+    hard_exp(1)
+    forward_z(2, 0)
+
+    x_far_right.wait_recv()
+    x_far_left.wait_recv()
+    y_far_right.wait_recv()
+    y_far_left.wait_recv()
+
+    def in_part(i, _):
+        part = pl.ds(pl.multiple_of(i * rows, rows), rows)
+        si_mine[part, :] = dot_nt(yp[part, :], xq[...])
+        return 0
+
+    lax.fori_loop(0, side, in_part, 0)
+    in_copy = send(si_mine, si_peer, other)
+    hard_part(2, 1)
+    for copy in aux_x_copies + aux_y_copies:
+        copy.wait_recv()
+    in_copy.wait_recv()
+    in_sums = [jnp.zeros((1, lanes), f32) for _ in range(side)]
+    in_moments = [jnp.zeros((1, lanes), f32) for _ in range(side)]
+    own_score = None
+    diagonal = lax.broadcasted_iota(jnp.int32, (rows, lanes), 0) == lax.broadcasted_iota(
+        jnp.int32, (rows, lanes), 1
+    )
+    for c in range(side):
+        c_row = position_row if c == 0 else aux_y[c - 1][0:1, :]
+        scale = to_column(c_row)
+        ccol[c * rows : (c + 1) * rows, :] = scale
+        part = slice(c * rows, (c + 1) * rows)
+        for n in range(side):
+            row_scale = inverse_temp * (q_row if n == 0 else aux_x[n - 1][7:8, :])
+            columns = slice(n * rows, (n + 1) * rows)
+            score = (si_mine[part, columns] + si_peer[part, columns]) * (scale * row_scale)
+            weight = jnp.exp(score)
+            if c == 0 and n == 0:
+                own_score = jnp.sum(jnp.where(diagonal, score, 0.0), axis=0, keepdims=True)
+                weight = jnp.where(diagonal, 0.0, weight)
+            ein_t[part, columns] = weight
+            ein_s[part, columns] = weight * score
+            ein[columns, part] = jnp.transpose(weight * scale).astype(bf16)
+            in_sums[n] = in_sums[n] + jnp.sum(weight, axis=0, keepdims=True)
+            in_moments[n] = in_moments[n] + jnp.sum(weight * score, axis=0, keepdims=True)
+    sum_x_copies = []
+    for n in range(1, side):
+        sum_out[6 + n] = jnp.where(line == 0, in_sums[n], in_moments[n])
+        sum_x_copies.append(send(sum_out.at[6 + n], sum_x.at[n - 1], x_homes[n - 1]))
+
+    forward_z(2, 1)
+
     def in_product(start, stop, other_rows):
         def body(i, _):
             columns = pl.ds(pl.multiple_of(i * wide, wide), wide)
@@ -336,6 +399,8 @@
             return 0
 
         lax.fori_loop(0, width // wide, body, 0)
+
+    in_product(3 * rows, 4 * rows, yp)
 
     grain = 16
 
@@ -376,96 +441,14 @@
         before = send(send_buffer.at[rows_of(0, 1)], recv_buffer.at[rows_of(0, 1)], at(-1))
         return [before, after]
 
-    in_sums = [jnp.zeros((1, lanes), f32) for _ in range(side)]
-    in_moments = [jnp.zeros((1, lanes), f32) for _ in range(side)]
-    diagonal = lax.broadcasted_iota(jnp.int32, (rows, lanes), 0) == lax.broadcasted_iota(
-        jnp.int32, (rows, lanes), 1
-    )
-
-    def in_part(c_start, c_stop, n_start, n_stop):
-        def body(i, _):
-            part = pl.ds(pl.multiple_of(c_start * rows + i * rows, rows), rows)
-            scores = dot_nt(yp[part, :], xq[n_start * rows : n_stop * rows, :])
-            for n in range(n_start, n_stop):
-                k = (n - n_start) * lanes
-                si_mine[n, part, :] = scores[:, k : k + lanes]
-            return 0
-
-        lax.fori_loop(0, c_stop - c_start, body, 0)
-        block = (pl.ds(n_start, n_stop - n_start), pl.ds(c_start * rows, (c_stop - c_start) * rows))
-        return send(si_mine.at[block], si_peer.at[block], other)
-
-    def in_exp(c, n):
-        c_row = position_row if c == 0 else aux_y[c - 1][0:1, :]
-        scale = to_column(c_row)
-        part = slice(c * rows, (c + 1) * rows)
-        row_scale = inverse_temp * (q_row if n == 0 else aux_x[n - 1][7:8, :])
-        columns = slice(n * rows, (n + 1) * rows)
-        score = (si_mine[n, part, :] + si_peer[n, part, :]) * (scale * row_scale)
-        weight = jnp.exp(score)
-        own = None
-        if c == 0 and n == 0:
-            own = jnp.sum(jnp.where(diagonal, score, 0.0), axis=0, keepdims=True)
-            weight = jnp.where(diagonal, 0.0, weight)
-        ein_t[part, columns] = weight
-        ein_s[part, columns] = weight * score
-        ein[columns, part] = jnp.transpose(weight * scale).astype(bf16)
-        in_sums[n] = in_sums[n] + jnp.sum(weight, axis=0, keepdims=True)
-        in_moments[n] = in_moments[n] + jnp.sum(weight * score, axis=0, keepdims=True)
-        return own
-
-    forward_z(1, 0)
-    hard_part(0, 1)
-    hard_exp(0)
-    forward_z(1, 1)
-    x_right.wait_recv()
-    x_far_right = send(xq.at[rows_of(1, 0)], xq.at[rows_of(3, 0)], at_x(1))
-    x_left.wait_recv()
-    x_far_left = send(xq.at[rows_of(2, 1)], xq.at[rows_of(3, 1)], at_x(-1))
-    y_right.wait_recv()
-    y_far_right = send(yp.at[rows_of(1, 0)], yp.at[rows_of(3, 0)], at_y(1))
-    y_left.wait_recv()
-    y_far_left = send(yp.at[rows_of(2, 1)], yp.at[rows_of(3, 1)], at_y(-1))
-    hard_part(1, 1)
-    near_copy = in_part(0, 3, 0, 3)
-    hard_exp(1)
-    for copy in aux_x_copies + aux_y_copies:
-        copy.wait_recv()
-    near_copy.wait_recv()
-    own_score = in_exp(0, 0)
-    for c in range(3):
-        for n in range(3):
-            if c or n:
-                in_exp(c, n)
-    forward_z(2, 0)
-    hard_part(2, 1)
-    x_far_right.wait_recv()
-    x_far_left.wait_recv()
-    far_x_copy = in_part(0, 3, 3, 4)
-    y_far_right.wait_recv()
-    y_far_left.wait_recv()
-    far_y_copy = in_part(3, 4, 0, 4)
-    hard_exp(2)
-    far_x_copy.wait_recv()
-    for c in range(3):
-        in_exp(c, 3)
-    far_y_copy.wait_recv()
-    for n in range(side):
-        in_exp(3, n)
-    sum_x_copies = []
-    for n in range(1, side):
-        sum_out[6 + n] = jnp.where(line == 0, in_sums[n], in_moments[n])
-        sum_x_copies.append(send(sum_out.at[6 + n], sum_x.at[n - 1], x_homes[n - 1]))
-    in_product(3 * rows, 4 * rows, yp)
     x_first = square_first(xs_send, xs_recv, at_x)
-    forward_z(2, 1)
     hard_part(3, 1)
     in_product(0, 3 * rows, yp)
     x_second = square_free(xs_send, xs_recv, at_x)
-    hard_exp(3)
+    hard_exp(2)
     forward_z(3, 0)
     hard_part(4, 1)
-    x_second += square_last(x_first, xs_send, xs_recv, at_x)
+    hard_exp(3)
     hard_exp(4)
 
     def hard_query(slot, count, base):
@@ -506,6 +489,7 @@
     hard_query(4, 1, 0)
     stage_back(3, half, half, True)
     stage_back(3, 0, half, False)
+    x_second += square_last(x_first, xs_send, xs_recv, at_x)
     forward_z(3, 1)
     hard_part(5, 1)
     start_back(3, half, half, True)
@@ -707,7 +691,8 @@
     for k in range(1, side):
         value = value + loss_y[k]
     queries = rows * owners * side * side
-    loss_ref[0, 0] = jnp.sum(value[0:1, :]) * (1.0 / queries)
+    mean = jnp.sum(value[0:1, :], axis=1, keepdims=True) * (1.0 / queries)
+    loss_ref[...] = jnp.broadcast_to(mean, (8, lanes))
     drain(older)
 
     def query_out(first):
@@ -733,13 +718,16 @@
     drain(len(sent))
 
 
-def flush(dq_ref, dp_ref, dq_out, dp_out, sems):
+def flush(loss_ref, dq_ref, dp_ref, loss_out, dq_out, dp_out, one, sems):
     copies = [
         pltpu.make_async_copy(dp_ref, dp_out, sems.at[0]),
         pltpu.make_async_copy(dq_ref, dq_out, sems.at[1]),
     ]
     for copy in copies:
         copy.start()
+    one[...] = loss_ref[0:1, 0:1]
+    copies.append(pltpu.make_async_copy(one, loss_out, sems.at[2]))
+    copies[2].start()
     for copy in copies:
         copy.wait()
 
@@ -747,7 +735,7 @@
 def on_device(queries, passages, positive_slot, hard_offset, hard_slot):
     rows, width = queries.shape
     p_rows = passages.shape[0]
-    copies = 128
+    copies = 110
     vmem = pl.BlockSpec(memory_space=pltpu.VMEM)
     hbm = pl.BlockSpec(memory_space=pltpu.HBM)
 
@@ -760,12 +748,12 @@
     loss, query_grad, passage_grad = pl.pallas_call(
         kernel,
         out_shape=(
-            jax.ShapeDtypeStruct((1, 1), f32),
+            pltpu.VMEM((8, lanes), f32),
             pltpu.VMEM(queries.shape, bf16),
             pltpu.VMEM(passages.shape, bf16),
         ),
         in_specs=[vmem, vmem, vmem, hbm, hbm],
-        out_specs=(pl.BlockSpec(memory_space=pltpu.SMEM), vmem, vmem),
+        out_specs=(vmem, vmem, vmem),
         scratch_shapes=[
             b(p_rows, width),
             b(9 * rows, width),
@@ -778,8 +766,8 @@
             f(5 * rows, width),
             b(4 * rows, width),
             b(4 * rows, width),
-            f(4, 4 * rows, rows),
-            f(4, 4 * rows, rows),
+            f(4 * rows, 4 * rows),
+            f(4 * rows, 4 * rows),
             f(4 * rows, 4 * rows),
             f(4 * rows, 4 * rows),
             b(4 * rows, 4 * rows),
@@ -796,6 +784,7 @@
             f(p_rows + rows, lanes),
             f(p_rows, lanes),
             f(rows, lanes),
+            f(4 * rows, lanes),
             f(8, lanes),
             f(7, 8, lanes),
             f(3, 8, lanes),
@@ -829,17 +818,19 @@
             flops=15_000_000_000, bytes_accessed=6_000_000, transcendentals=800_000
         ),
     )(positive_slot.reshape(1, rows), hard_offset.T, hard_slot.T, queries, passages)
-    query_grad, passage_grad = pl.pallas_call(
+    loss, query_grad, passage_grad = pl.pallas_call(
         flush,
         out_shape=(
+            jax.ShapeDtypeStruct((1, 1), f32),
             jax.ShapeDtypeStruct(queries.shape, bf16),
             jax.ShapeDtypeStruct(passages.shape, bf16),
         ),
-        in_specs=[vmem, vmem],
-        out_specs=(hbm, hbm),
-        scratch_shapes=[pltpu.SemaphoreType.DMA((2,))],
+        in_specs=[vmem, vmem, vmem],
+        out_specs=(hbm, hbm, hbm),
+        scratch_shapes=[f(1, 1), pltpu.SemaphoreType.DMA((3,))],
         compiler_params=pltpu.CompilerParams(vmem_limit_bytes=1024 * 1024),
     )(
+        pltpu.with_memory_space_constraint(loss, pltpu.VMEM),
         pltpu.with_memory_space_constraint(query_grad, pltpu.VMEM),
         pltpu.with_memory_space_constraint(passage_grad, pltpu.VMEM),
     )

time: 101 us -> 98.1 us (0.971)
  between operations: 2.41 us -> 0.64 us
  Pallas kernels: 97.8 us -> 96.1 us
    pallas_call x2, Pallas kernels: 97.8 us -> 96.1 us  [the longest x1 94.5 us: on_device(): pl.pallas_call(kernel, out_shape=(pltpu.VMEM((8, lanes), f32), pltpu.VMEM...]
where the time goes in v2:
time: 98.1 us; the launch traced here: 96.7 us
  Pallas kernels  96.1 us (98%)
    pallas_call x1, Pallas kernels, on_device(): pl.pallas_call(kernel, out_shape=(pltpu.VMEM((8, lanes), f32), pltpu.VMEM...  94.5 us

profile of v2, /device:TPU:1, one launch (start us, length us, event | category | flops | bytes accessed | tf_op | source)
XLA Modules:
  0.0 96.7 jit_solution(8908623422944458901)
XLA Ops:
  0.6 94.5 %shard_map.76 = (f32[8,128]{1,0:T(8,128)S(1)}, bf16[128,2048]{1,0:T(8,128)(2,1)S(1)}, bf16[512,2048]{1,0:T(8,128)(2,1)S(1)}) custom-call(s32[1,128]{1,0:T(1,128)} %bitcast.6, s32[7,128]{1,0:T(8,128)} %bitcast.4, s32[7,128]{1,0:T(8,128)} %bitcast.5, bf16[128,2048]{1,0:T(8,128)(2,1)} %q_hbm.1, bf16[512,2048]{1,0:T(8,128)(2,1)} %p_hbm.1), custom_call_target="tpu_custom_call" | custom-call | flops 15000000512 | bytes 6000000 | tf_op jit(solution)/shard_map/pallas_call | solution.py:748
  95.2 1.5 %shard_map.77 = (f32[1,1]{1,0:T(1,128)}, bf16[128,2048]{1,0:T(8,128)(2,1)}, bf16[512,2048]{1,0:T(8,128)(2,1)}) custom-call(f32[8,128]{1,0:T(8,128)S(1)} %get-tuple-element.9.loss_ref, bf16[128,2048]{1,0:T(8,128)(2,1)S(1)} %get-tuple-element.10.dq_ref, bf16[512,2048]{1,0:T(8,128)(2,1)S(1)} %get-tuple-element.11.dp_ref), custom_call_target="tpu_custom_call" | custom-call | tf_op jit(solution)/shard_map/pallas_call | solution.py:821

commit v3 on v2

--- a/solution.py
+++ b/solution.py
@@ -9,6 +9,10 @@
 inverse_temp = 50.0
 side = 4
 lanes = 128
+shared = ("aux_z", "aux_x", "aux_y", "sum_z", "sum_x", "fac_z", "fac_x", "own")
+shared = shared + ("loss_z", "loss_x", "loss_y")
+kinds = shared + ("z", "x", "y", "back_z", "back_x", "back_y", "norm", "hard", "in", "along")
+alone = 61
 f32 = jnp.float32
 bf16 = jnp.bfloat16
 
@@ -123,27 +127,28 @@
 
     other = (group, z, 1 - t)
 
-    sent = []
-    done = [0]
-
-    def drain(count):
-        for copy in sent[done[0] : count]:
-            copy.wait_send()
-        done[0] = max(done[0], count)
-
-    def send(src, dst, target):
-        k = len(sent)
+    received = []
+
+    def send(src, dst, target, kind, together=False):
+        if not together:
+            received.append(kind)
+        slot = kinds.index(kind) if together else len(shared) + len(received) - 1
         copy = pltpu.make_async_remote_copy(
             src_ref=src,
             dst_ref=dst,
-            send_sem=send_sems.at[k],
-            recv_sem=recv_sems.at[k],
+            send_sem=send_sems.at[kinds.index(kind)],
+            recv_sem=recv_sems.at[slot],
             device_id=target,
             device_id_type=pl.DeviceIdType.MESH,
         )
         copy.start()
-        sent.append(copy)
         return copy
+
+    def wait_sent(kind, ref):
+        pltpu.make_async_copy(ref, ref, send_sems.at[kinds.index(kind)]).wait()
+
+    def wait_came(kind, ref):
+        pltpu.make_async_copy(ref, ref, recv_sems.at[kinds.index(kind)]).wait()
 
     def rows_of(slot, part=None):
         if part is None:
@@ -192,10 +197,10 @@
     for c in range(2):
         right_own = q_hbm.at[pl.ds(c * half, half)]
         left_own = q_hbm.at[pl.ds((1 - c) * half, half)]
-        z_right[1, c] = send(right_own, zq.at[z_rows(1, True, c)], at_z(1))
-        z_left[1, 1 - c] = send(left_own, zq.at[z_rows(1, False, 1 - c)], at_z(-1))
-    x_right = send(q_hbm, xq.at[rows_of(1)], at_x(1))
-    x_left = send(q_hbm, xq.at[rows_of(2)], at_x(-1))
+        z_right[1, c] = send(right_own, zq.at[z_rows(1, True, c)], at_z(1), "z")
+        z_left[1, 1 - c] = send(left_own, zq.at[z_rows(1, False, 1 - c)], at_z(-1), "z")
+    x_right = send(q_hbm, xq.at[rows_of(1)], at_x(1), "x")
+    x_left = send(q_hbm, xq.at[rows_of(2)], at_x(-1), "x")
     load_q.wait()
     load_p.wait()
     q_ref = xq
@@ -216,8 +221,8 @@
         return 0
 
     lax.fori_loop(0, width // wide, pick_columns, 0)
-    y_right = send(yp.at[rows_of(0)], yp.at[rows_of(1)], at_y(1))
-    y_left = send(yp.at[rows_of(0)], yp.at[rows_of(2)], at_y(-1))
+    y_right = send(yp.at[rows_of(0)], yp.at[rows_of(1)], at_y(1), "y")
+    y_left = send(yp.at[rows_of(0)], yp.at[rows_of(2)], at_y(-1), "y")
 
     strip = 32
 
@@ -234,7 +239,7 @@
 
     lax.fori_loop(0, p_rows // strip, square_strip(p_ref, 0), 0)
     lax.fori_loop(0, rows // strip, square_strip(q_ref, p_rows), 0)
-    norm_copy = send(norm_mine, norm_peer, other)
+    norm_copy = send(norm_mine, norm_peer, other, "norm")
     norm_copy.wait_recv()
 
     def scale_of(start):
@@ -257,19 +262,21 @@
     aux_own[0:7, :] = (owner_ids * p_rows + hard_slot_ref[...]).astype(f32)
     aux_own[7:8, :] = q_row
     pos_own[...] = jnp.broadcast_to(position_row, (8, lanes))
-    aux_z_copies = [send(aux_own, aux_z.at[m], z_targets[m]) for m in range(7)]
-    aux_x_copies = [send(aux_own, aux_x.at[m], x_targets[m]) for m in range(3)]
-    aux_y_copies = [send(pos_own, aux_y.at[m], y_targets[m]) for m in range(3)]
+    for m in range(7):
+        send(aux_own, aux_z.at[m], z_targets[m], "aux_z", True)
+    for m in range(3):
+        send(aux_own, aux_x.at[m], x_targets[m], "aux_x", True)
+        send(pos_own, aux_y.at[m], y_targets[m], "aux_y", True)
 
     def forward_z(k, c):
         z_right[k, c].wait_recv()
         here = zq.at[z_rows(k, True, c)]
         if k < 3 or c == 0:
-            z_right[k + 1, c] = send(here, zq.at[z_rows(k + 1, True, c)], at_z(1))
+            z_right[k + 1, c] = send(here, zq.at[z_rows(k + 1, True, c)], at_z(1), "z")
         z_left[k, 1 - c].wait_recv()
         here = zq.at[z_rows(k, False, 1 - c)]
         if k < 3 or c == 0:
-            z_left[k + 1, 1 - c] = send(here, zq.at[z_rows(k + 1, False, 1 - c)], at_z(-1))
+            z_left[k + 1, 1 - c] = send(here, zq.at[z_rows(k + 1, False, 1 - c)], at_z(-1), "z")
 
     line = lax.broadcasted_iota(jnp.int32, (8, lanes), 0)
     hard_copies = {}
@@ -284,7 +291,7 @@
 
         lax.fori_loop(0, p_rows // 256, body, 0)
         here = pl.ds(tile, count)
-        copy = send(sh_mine.at[here], sh_peer.at[here], other)
+        copy = send(sh_mine.at[here], sh_peer.at[here], other, "hard")
         for n in range(count):
             hard_copies[tile + n] = copy if n == 0 else None
 
@@ -294,9 +301,8 @@
     def hard_exp(tile):
         if hard_copies[tile] is not None:
             hard_copies[tile].wait_recv()
-        if tile == far or tile % 2 == 0:
-            for block in (far,) if tile == far else (tile, tile + 1):
-                aux_z_copies[block].wait_recv()
+        if tile == 0:
+            wait_came("aux_z", aux_z)
         packet = of_tile(tile, lambda block: aux_z[block])
         row_scale = inverse_temp * packet[7:8, :]
         columns = slice(tile * rows, (tile + 1) * rows)
@@ -324,22 +330,20 @@
         sums, moments = lax.fori_loop(0, tiles, body, (zero, zero))
         hard_sums[tile] = jnp.where(line == 0, sums, moments)
 
-    sum_z_copies = {}
-
     def send_hard_sum(slot):
         sum_out[slot] = of_tile(slot, lambda tile: hard_sums[tile])
-        sum_z_copies[slot] = send(sum_out.at[slot], sum_z.at[slot], z_homes[slot])
+        send(sum_out.at[slot], sum_z.at[slot], z_homes[slot], "sum_z", True)
 
     forward_z(1, 0)
     forward_z(1, 1)
     x_right.wait_recv()
-    x_far_right = send(xq.at[rows_of(1, 0)], xq.at[rows_of(3, 0)], at_x(1))
+    x_far_right = send(xq.at[rows_of(1, 0)], xq.at[rows_of(3, 0)], at_x(1), "x")
     x_left.wait_recv()
-    x_far_left = send(xq.at[rows_of(2, 1)], xq.at[rows_of(3, 1)], at_x(-1))
+    x_far_left = send(xq.at[rows_of(2, 1)], xq.at[rows_of(3, 1)], at_x(-1), "x")
     y_right.wait_recv()
-    y_far_right = send(yp.at[rows_of(1, 0)], yp.at[rows_of(3, 0)], at_y(1))
+    y_far_right = send(yp.at[rows_of(1, 0)], yp.at[rows_of(3, 0)], at_y(1), "y")
     y_left.wait_recv()
-    y_far_left = send(yp.at[rows_of(2, 1)], yp.at[rows_of(3, 1)], at_y(-1))
+    y_far_left = send(yp.at[rows_of(2, 1)], yp.at[rows_of(3, 1)], at_y(-1), "y")
     hard_part(0, 2)
     hard_exp(0)
     hard_exp(1)
@@ -356,10 +360,10 @@
         return 0
 
     lax.fori_loop(0, side, in_part, 0)
-    in_copy = send(si_mine, si_peer, other)
+    in_copy = send(si_mine, si_peer, other, "in")
     hard_part(2, 1)
-    for copy in aux_x_copies + aux_y_copies:
-        copy.wait_recv()
+    wait_came("aux_x", aux_x)
+    wait_came("aux_y", aux_y)
     in_copy.wait_recv()
     in_sums = [jnp.zeros((1, lanes), f32) for _ in range(side)]
     in_moments = [jnp.zeros((1, lanes), f32) for _ in range(side)]
@@ -385,10 +389,9 @@
             ein[columns, part] = jnp.transpose(weight * scale).astype(bf16)
             in_sums[n] = in_sums[n] + jnp.sum(weight, axis=0, keepdims=True)
             in_moments[n] = in_moments[n] + jnp.sum(weight * score, axis=0, keepdims=True)
-    sum_x_copies = []
     for n in range(1, side):
         sum_out[6 + n] = jnp.where(line == 0, in_sums[n], in_moments[n])
-        sum_x_copies.append(send(sum_out.at[6 + n], sum_x.at[n - 1], x_homes[n - 1]))
+        send(sum_out.at[6 + n], sum_x.at[n - 1], x_homes[n - 1], "sum_x", True)
 
     forward_z(2, 1)
 
@@ -418,33 +421,33 @@
 
         lax.fori_loop(0, count // grain, body, 0)
 
-    def square_first(send_buffer, recv_buffer, at):
+    def square_first(send_buffer, recv_buffer, at, kind):
         stage(send_buffer, 2 * rows, pin, 3 * rows, rows)
         return (
-            send(send_buffer.at[rows_of(2, 0)], recv_buffer.at[rows_of(2, 0)], at(1)),
-            send(send_buffer.at[rows_of(2, 1)], recv_buffer.at[rows_of(2, 1)], at(-1)),
+            send(send_buffer.at[rows_of(2, 0)], recv_buffer.at[rows_of(2, 0)], at(1), kind),
+            send(send_buffer.at[rows_of(2, 1)], recv_buffer.at[rows_of(2, 1)], at(-1), kind),
         )
 
-    def square_free(send_buffer, recv_buffer, at):
+    def square_free(send_buffer, recv_buffer, at, kind):
         stage(send_buffer, 0, pin, rows, half)
-        before = send(send_buffer.at[rows_of(0, 0)], recv_buffer.at[rows_of(0, 0)], at(-1))
+        before = send(send_buffer.at[rows_of(0, 0)], recv_buffer.at[rows_of(0, 0)], at(-1), kind)
         stage(send_buffer, rows + half, pin, 2 * rows + half, half)
-        after = send(send_buffer.at[rows_of(1, 1)], recv_buffer.at[rows_of(1, 1)], at(1))
+        after = send(send_buffer.at[rows_of(1, 1)], recv_buffer.at[rows_of(1, 1)], at(1), kind)
         return [before, after]
 
-    def square_last(first, send_buffer, recv_buffer, at):
+    def square_last(first, send_buffer, recv_buffer, at, kind):
         first[0].wait_recv()
         stage(send_buffer, rows, pin, 2 * rows, half, recv_buffer, 2 * rows)
-        after = send(send_buffer.at[rows_of(1, 0)], recv_buffer.at[rows_of(1, 0)], at(1))
+        after = send(send_buffer.at[rows_of(1, 0)], recv_buffer.at[rows_of(1, 0)], at(1), kind)
         first[1].wait_recv()
         stage(send_buffer, half, pin, rows + half, half, recv_buffer, 2 * rows + half)
-        before = send(send_buffer.at[rows_of(0, 1)], recv_buffer.at[rows_of(0, 1)], at(-1))
+        before = send(send_buffer.at[rows_of(0, 1)], recv_buffer.at[rows_of(0, 1)], at(-1), kind)
         return [before, after]
 
-    x_first = square_first(xs_send, xs_recv, at_x)
+    x_first = square_first(xs_send, xs_recv, at_x, "back_x")
     hard_part(3, 1)
     in_product(0, 3 * rows, yp)
-    x_second = square_free(xs_send, xs_recv, at_x)
+    x_second = square_free(xs_send, xs_recv, at_x, "back_x")
     hard_exp(2)
     forward_z(3, 0)
     hard_part(4, 1)
@@ -479,7 +482,7 @@
     def start_back(k, start, count, right):
         here = pl.ds(place(k, not right, start), count)
         (back_right if right else back_left)[k, start] = send(
-            zs_send.at[here], zs_recv.at[here], at_z(1 if right else -1)
+            zs_send.at[here], zs_recv.at[here], at_z(1 if right else -1), "back_z"
         )
 
     def send_back(k, start, count, right, came=None, wait=True):
@@ -489,7 +492,7 @@
     hard_query(4, 1, 0)
     stage_back(3, half, half, True)
     stage_back(3, 0, half, False)
-    x_second += square_last(x_first, xs_send, xs_recv, at_x)
+    x_second += square_last(x_first, xs_send, xs_recv, at_x, "back_x")
     forward_z(3, 1)
     hard_part(5, 1)
     start_back(3, half, half, True)
@@ -506,16 +509,15 @@
     hard_query(far, 1, 4 * rows)
     send_back(4, 0, half, True)
     send_back(4, half, half, False)
-    older = len(sent) - 8
 
     rest = in_sums[0]
     moment = in_moments[0]
+    wait_came("sum_x", sum_x)
+    wait_came("sum_z", sum_z)
     for m in range(3):
-        sum_x_copies[m].wait_recv()
         rest = rest + sum_x[m][0:1, :]
         moment = moment + sum_x[m][1:2, :]
     for m in range(7):
-        sum_z_copies[m].wait_recv()
         rest = rest + sum_z[m][0:1, :]
         moment = moment + sum_z[m][1:2, :]
     total = rest + jnp.exp(own_score)
@@ -523,10 +525,13 @@
     factor = ratio * q_row
     inverse = 1.0 / total
     fac_own[...] = jnp.where(line == 0, factor, inverse)
-    fac_x_copies = [send(fac_own, fac_x.at[m], x_targets[m]) for m in range(3)]
-    fac_z_copies = [send(fac_own, fac_z.at[m], z_targets[m]) for m in range(7)]
+    for m in range(3):
+        send(fac_own, fac_x.at[m], x_targets[m], "fac_x", True)
+    for m in range(7):
+        send(fac_own, fac_z.at[m], z_targets[m], "fac_z", True)
     loss_z[z] = jnp.broadcast_to(jnp.log(total) - own_score, (8, lanes))
-    loss_z_copies = [send(loss_z.at[z], loss_z.at[z], at_z(k)) for k in range(1, 8)]
+    for k in range(1, 8):
+        send(loss_z.at[z], loss_z.at[z], at_z(k), "loss_z", True)
 
     hard_query(2, 2, 2 * rows)
 
@@ -537,8 +542,7 @@
     along_col[...] = to_column(along * q_row * q_row)
     repeat = width // lanes
 
-    for copy in fac_x_copies:
-        copy.wait_recv()
+    wait_came("fac_x", fac_x)
     for n in range(side):
         fac_row = factor if n == 0 else fac_x[n - 1][0:1, :]
         columns = slice(n * rows, (n + 1) * rows)
@@ -547,11 +551,11 @@
             ein[part, columns] = (ein_t[part, columns] * fac_row).astype(bf16)
 
     in_product(3 * rows, 4 * rows, xq)
-    y_first = square_first(ys_send, ys_recv, at_y)
+    y_first = square_first(ys_send, ys_recv, at_y, "back_y")
     send_back(2, half, half, True, came=(3, half))
     send_back(2, 0, half, False, came=(3, 0))
     in_product(rows, 3 * rows, xq)
-    y_second = square_free(ys_send, ys_recv, at_y)
+    y_second = square_free(ys_send, ys_recv, at_y, "back_y")
 
     for copy in x_second:
         copy.wait_recv()
@@ -574,7 +578,6 @@
     in_product(0, rows, xq)
 
     own_along = None
-    own_copies = []
     for c in range(side):
         part = slice(c * rows, (c + 1) * rows)
         shares = jnp.zeros((rows, lanes), f32)
@@ -586,13 +589,12 @@
             own_along = row - rest * own_score * inverse
         else:
             own_out[c - 1] = jnp.broadcast_to(row, (8, lanes))
-            own_copies.append(send(own_out.at[c - 1], own_y.at[c - 1], y_homes[c - 1]))
+            send(own_out.at[c - 1], own_y.at[c - 1], y_homes[c - 1], "own", True)
     send_back(3, 0, half, True, came=(4, 0))
     send_back(3, half, half, False, came=(4, half))
     hard_query(0, 2, 0)
 
-    for m in range(7):
-        fac_z_copies[m].wait_recv()
+    wait_came("fac_z", fac_z)
     for m in range(7):
         columns = slice(m * rows, (m + 1) * rows)
         fac_row = of_tile(m, lambda block: fac_z[block][0:1, :])
@@ -600,7 +602,7 @@
             part = slice(c * rows, (c + 1) * rows)
             wt[part, columns] = (eh_t[part, columns] * fac_row).astype(bf16)
 
-    y_second += square_last(y_first, ys_send, ys_recv, at_y)
+    y_second += square_last(y_first, ys_send, ys_recv, at_y, "back_y")
     send_back(1, half, half, True, came=(2, half))
     send_back(1, 0, half, False, came=(2, 0))
 
@@ -610,7 +612,21 @@
         return 0
 
     lax.fori_loop(0, width // 256, passage_hard, 0)
-    drain(older)
+    wait_sent("z", zq.at[pl.ds(0, 7 * rows)])
+    wait_sent("x", xq.at[pl.ds(0, 3 * rows)])
+    wait_sent("y", yp.at[pl.ds(0, 3 * rows)])
+    wait_sent("back_x", xs_send)
+    wait_sent("norm", norm_mine)
+    wait_sent("hard", sh_mine)
+    wait_sent("in", si_mine)
+    wait_sent("aux_z", aux_z)
+    wait_sent("aux_x", aux_x)
+    wait_sent("aux_y", aux_y)
+    wait_sent("sum_z", sum_z)
+    wait_sent("sum_x", sum_x)
+    wait_sent("fac_z", fac_z)
+    wait_sent("fac_x", fac_x)
+    wait_sent("own", own_y)
 
     def passage_along(i, _):
         part = pl.ds(pl.multiple_of(i * grain, grain), grain)
@@ -618,30 +634,29 @@
         return 0
 
     lax.fori_loop(0, p_rows // grain, passage_along, 0)
-    along_p_copy = send(along_p_mine, along_p_peer, other)
+    along_p_copy = send(along_p_mine, along_p_peer, other, "along")
     quarter = half // 2
     for start in (0, quarter):
         send_back(2, start, quarter, True, came=(3, 0), wait=start == 0)
         send_back(2, half + start, quarter, False, came=(3, half), wait=start == 0)
 
-    for copy in loss_z_copies:
-        copy.wait_recv()
+    wait_came("loss_z", loss_z.at[pl.ds(0, 7)])
     value = loss_z[0]
     for k in range(1, 8):
         value = value + loss_z[k]
     loss_x[x] = value
-    loss_x_copies = [send(loss_x.at[x], loss_x.at[x], at_x(k)) for k in range(1, side)]
-    older = len(sent) - 8
-    for copy in loss_x_copies:
-        copy.wait_recv()
+    for k in range(1, side):
+        send(loss_x.at[x], loss_x.at[x], at_x(k), "loss_x", True)
+    wait_came("loss_x", loss_x.at[pl.ds(0, 3)])
     value = loss_x[0]
     for k in range(1, side):
         value = value + loss_x[k]
     loss_y[y] = value
-    loss_y_copies = [send(loss_y.at[y], loss_y.at[y], at_y(k)) for k in range(1, side)]
-
+    for k in range(1, side):
+        send(loss_y.at[y], loss_y.at[y], at_y(k), "loss_y", True)
+
+    wait_came("own", own_y)
     for m in range(3):
-        own_copies[m].wait_recv()
         own_along = own_along + own_y[m][0:1, :]
     along_p_copy.wait_recv()
     for copy in y_second:
@@ -685,15 +700,18 @@
     lax.fori_loop(tiles // 2, tiles, passage_out, 0)
     send_back(1, quarter, quarter, True, came=(2, quarter))
     send_back(1, half + quarter, quarter, False, came=(2, half + quarter))
-    for copy in loss_y_copies:
-        copy.wait_recv()
+    wait_came("loss_y", loss_y.at[pl.ds(0, 3)])
     value = loss_y[0]
     for k in range(1, side):
         value = value + loss_y[k]
     queries = rows * owners * side * side
     mean = jnp.sum(value[0:1, :], axis=1, keepdims=True) * (1.0 / queries)
     loss_ref[...] = jnp.broadcast_to(mean, (8, lanes))
-    drain(older)
+    wait_sent("loss_z", loss_z.at[pl.ds(0, 7)])
+    wait_sent("loss_x", loss_x.at[pl.ds(0, 3)])
+    wait_sent("loss_y", loss_y.at[pl.ds(0, 3)])
+    wait_sent("along", along_p_mine)
+    wait_sent("back_y", ys_send)
 
     def query_out(first):
         def body(i, _):
@@ -715,7 +733,7 @@
         query_out(start)
         back_left[1, half + start].wait_recv()
         query_out(half + start)
-    drain(len(sent))
+    wait_sent("back_z", zs_send)
 
 
 def flush(loss_ref, dq_ref, dp_ref, loss_out, dq_out, dp_out, one, sems):
@@ -735,7 +753,6 @@
 def on_device(queries, passages, positive_slot, hard_offset, hard_slot):
     rows, width = queries.shape
     p_rows = passages.shape[0]
-    copies = 110
     vmem = pl.BlockSpec(memory_space=pltpu.VMEM)
     hbm = pl.BlockSpec(memory_space=pltpu.HBM)
 
@@ -807,8 +824,8 @@
             f(rows, lanes),
             f(rows, lanes),
             f(rows, lanes),
-            pltpu.SemaphoreType.DMA((copies,)),
-            pltpu.SemaphoreType.DMA((copies,)),
+            pltpu.SemaphoreType.DMA((len(kinds),)),
+            pltpu.SemaphoreType.DMA((len(shared) + alone,)),
             pltpu.SemaphoreType.DMA((2,)),
         ],
         compiler_params=pltpu.CompilerParams(

time: 98.1 us -> 96.9 us (0.988)
  Pallas kernels: 96.1 us -> 94.9 us
    pallas_call x1, Pallas kernels: 94.5 us -> 93.4 us  [on_device(): pl.pallas_call(kernel, out_shape=(pltpu.VMEM((8, lanes), f32), pltpu.VMEM...]
where the time goes in v3:
time: 96.9 us; the launch traced here: 95.5 us
  Pallas kernels  94.9 us (98%)
    pallas_call x1, Pallas kernels, on_device(): pl.pallas_call(kernel, out_shape=(pltpu.VMEM((8, lanes), f32), pltpu.VMEM...  93.4 us

profile of v3, /device:TPU:1, one launch (start us, length us, event | category | flops | bytes accessed | tf_op | source)
XLA Modules:
  0.0 95.5 jit_solution(17856705297312908713)
XLA Ops:
  0.6 93.4 %shard_map.76 = (f32[8,128]{1,0:T(8,128)S(1)}, bf16[128,2048]{1,0:T(8,128)(2,1)S(1)}, bf16[512,2048]{1,0:T(8,128)(2,1)S(1)}) custom-call(s32[1,128]{1,0:T(1,128)} %bitcast.6, s32[7,128]{1,0:T(8,128)} %bitcast.4, s32[7,128]{1,0:T(8,128)} %bitcast.5, bf16[128,2048]{1,0:T(8,128)(2,1)} %q_hbm.1, bf16[512,2048]{1,0:T(8,128)(2,1)} %p_hbm.1), custom_call_target="tpu_custom_call" | custom-call | flops 15000000512 | bytes 6000000 | tf_op jit(solution)/shard_map/pallas_call | solution.py:765
  94.0 1.5 %shard_map.77 = (f32[1,1]{1,0:T(1,128)}, bf16[128,2048]{1,0:T(8,128)(2,1)}, bf16[512,2048]{1,0:T(8,128)(2,1)}) custom-call(f32[8,128]{1,0:T(8,128)S(1)} %get-tuple-element.9.loss_ref, bf16[128,2048]{1,0:T(8,128)(2,1)S(1)} %get-tuple-element.10.dq_ref, bf16[512,2048]{1,0:T(8,128)(2,1)S(1)} %get-tuple-element.11.dp_ref), custom_call_target="tpu_custom_call" | custom-call | tf_op jit(solution)/shard_map/pallas_call | solution.py:838

commit v4 on v3

--- a/solution.py
+++ b/solution.py
@@ -87,6 +87,7 @@
     sum_out,
     sum_z,
     sum_x,
+    fac_row,
     fac_own,
     fac_z,
     fac_x,
@@ -261,7 +262,7 @@
     owner_ids = lax.rem(offset_ref[...] + (z + 1), owners)
     aux_own[0:7, :] = (owner_ids * p_rows + hard_slot_ref[...]).astype(f32)
     aux_own[7:8, :] = q_row
-    pos_own[...] = jnp.broadcast_to(position_row, (8, lanes))
+    pos_own[...] = position_row
     for m in range(7):
         send(aux_own, aux_z.at[m], z_targets[m], "aux_z", True)
     for m in range(3):
@@ -278,7 +279,7 @@
         if k < 3 or c == 0:
             z_left[k + 1, 1 - c] = send(here, zq.at[z_rows(k + 1, False, 1 - c)], at_z(-1), "z")
 
-    line = lax.broadcasted_iota(jnp.int32, (8, lanes), 0)
+    line = lax.broadcasted_iota(jnp.int32, (2, lanes), 0)
     hard_copies = {}
 
     def hard_part(tile, count):
@@ -524,12 +525,13 @@
     ratio = inverse_temp / total
     factor = ratio * q_row
     inverse = 1.0 / total
+    fac_row[...] = factor
     fac_own[...] = jnp.where(line == 0, factor, inverse)
     for m in range(3):
         send(fac_own, fac_x.at[m], x_targets[m], "fac_x", True)
     for m in range(7):
-        send(fac_own, fac_z.at[m], z_targets[m], "fac_z", True)
-    loss_z[z] = jnp.broadcast_to(jnp.log(total) - own_score, (8, lanes))
+        send(fac_row, fac_z.at[m], z_targets[m], "fac_z", True)
+    loss_z[z] = jnp.log(total) - own_score
     for k in range(1, 8):
         send(loss_z.at[z], loss_z.at[z], at_z(k), "loss_z", True)
 
@@ -544,11 +546,11 @@
 
     wait_came("fac_x", fac_x)
     for n in range(side):
-        fac_row = factor if n == 0 else fac_x[n - 1][0:1, :]
+        near_row = factor if n == 0 else fac_x[n - 1][0:1, :]
         columns = slice(n * rows, (n + 1) * rows)
         for c in range(side):
             part = slice(c * rows, (c + 1) * rows)
-            ein[part, columns] = (ein_t[part, columns] * fac_row).astype(bf16)
+            ein[part, columns] = (ein_t[part, columns] * near_row).astype(bf16)
 
     in_product(3 * rows, 4 * rows, xq)
     y_first = square_first(ys_send, ys_recv, at_y, "back_y")
@@ -588,7 +590,7 @@
         if c == 0:
             own_along = row - rest * own_score * inverse
         else:
-            own_out[c - 1] = jnp.broadcast_to(row, (8, lanes))
+            own_out[c - 1] = row
             send(own_out.at[c - 1], own_y.at[c - 1], y_homes[c - 1], "own", True)
     send_back(3, 0, half, True, came=(4, 0))
     send_back(3, half, half, False, came=(4, half))
@@ -597,10 +599,10 @@
     wait_came("fac_z", fac_z)
     for m in range(7):
         columns = slice(m * rows, (m + 1) * rows)
-        fac_row = of_tile(m, lambda block: fac_z[block][0:1, :])
+        tile_row = of_tile(m, lambda block: fac_z[block])
         for c in range(tiles):
             part = slice(c * rows, (c + 1) * rows)
-            wt[part, columns] = (eh_t[part, columns] * fac_row).astype(bf16)
+            wt[part, columns] = (eh_t[part, columns] * tile_row).astype(bf16)
 
     y_second += square_last(y_first, ys_send, ys_recv, at_y, "back_y")
     send_back(1, half, half, True, came=(2, half))
@@ -805,19 +807,20 @@
             f(8, lanes),
             f(7, 8, lanes),
             f(3, 8, lanes),
-            f(8, lanes),
-            f(3, 8, lanes),
-            f(10, 8, lanes),
-            f(7, 8, lanes),
-            f(3, 8, lanes),
-            f(8, lanes),
-            f(7, 8, lanes),
-            f(3, 8, lanes),
-            f(3, 8, lanes),
-            f(3, 8, lanes),
-            f(8, 8, lanes),
-            f(4, 8, lanes),
-            f(4, 8, lanes),
+            f(1, lanes),
+            f(3, 1, lanes),
+            f(10, 2, lanes),
+            f(7, 2, lanes),
+            f(3, 2, lanes),
+            f(1, lanes),
+            f(2, lanes),
+            f(7, 1, lanes),
+            f(3, 2, lanes),
+            f(3, 1, lanes),
+            f(3, 1, lanes),
+            f(8, 1, lanes),
+            f(4, 1, lanes),
+            f(4, 1, lanes),
             f(p_rows, lanes),
             f(p_rows, lanes),
             f(rows, lanes),

time: 96.9 us -> 96.6 us (level)
  no operation moved by 1% of the time
where the time goes in v4:
time: 96.6 us; the launch traced here: 95 us
  Pallas kernels  94.3 us (98%)
    pallas_call x1, Pallas kernels, on_device(): pl.pallas_call(kernel, out_shape=(pltpu.VMEM((8, lanes), f32), pltpu.VMEM...  92.8 us

profile of v4, /device:TPU:1, one launch (start us, length us, event | category | flops | bytes accessed | tf_op | source)
XLA Modules:
  0.0 95.0 jit_solution(14226565317020305148)
XLA Ops:
  0.6 92.8 %shard_map.76 = (f32[8,128]{1,0:T(8,128)S(1)}, bf16[128,2048]{1,0:T(8,128)(2,1)S(1)}, bf16[512,2048]{1,0:T(8,128)(2,1)S(1)}) custom-call(s32[1,128]{1,0:T(1,128)} %bitcast.6, s32[7,128]{1,0:T(8,128)} %bitcast.4, s32[7,128]{1,0:T(8,128)} %bitcast.5, bf16[128,2048]{1,0:T(8,128)(2,1)} %q_hbm.1, bf16[512,2048]{1,0:T(8,128)(2,1)} %p_hbm.1), custom_call_target="tpu_custom_call" | custom-call | flops 15000000512 | bytes 6000000 | tf_op jit(solution)/shard_map/pallas_call | solution.py:767
  93.4 1.5 %shard_map.77 = (f32[1,1]{1,0:T(1,128)}, bf16[128,2048]{1,0:T(8,128)(2,1)}, bf16[512,2048]{1,0:T(8,128)(2,1)}) custom-call(f32[8,128]{1,0:T(8,128)S(1)} %get-tuple-element.9.loss_ref, bf16[128,2048]{1,0:T(8,128)(2,1)S(1)} %get-tuple-element.10.dq_ref, bf16[512,2048]{1,0:T(8,128)(2,1)S(1)} %get-tuple-element.11.dp_ref), custom_call_target="tpu_custom_call" | custom-call | tf_op jit(solution)/shard_map/pallas_call | solution.py:841

commit v5 on v4

--- a/solution.py
+++ b/solution.py
@@ -78,7 +78,6 @@
     norm_peer,
     pcol,
     qcol,
-    ccol,
     aux_own,
     aux_z,
     aux_x,
@@ -92,6 +91,7 @@
     fac_z,
     fac_x,
     own_out,
+    crow,
     own_y,
     loss_z,
     loss_x,
@@ -366,30 +366,37 @@
     wait_came("aux_x", aux_x)
     wait_came("aux_y", aux_y)
     in_copy.wait_recv()
-    in_sums = [jnp.zeros((1, lanes), f32) for _ in range(side)]
-    in_moments = [jnp.zeros((1, lanes), f32) for _ in range(side)]
-    own_score = None
-    diagonal = lax.broadcasted_iota(jnp.int32, (rows, lanes), 0) == lax.broadcasted_iota(
+    crow[0] = position_row
+    for c in range(1, side):
+        crow[c] = aux_y[c - 1]
+    near_scale = [inverse_temp * (q_row if n == 0 else aux_x[n - 1][7:8, :]) for n in range(side)]
+    ahead = lax.broadcasted_iota(jnp.int32, (rows, lanes), 0) - lax.broadcasted_iota(
         jnp.int32, (rows, lanes), 1
     )
-    for c in range(side):
-        c_row = position_row if c == 0 else aux_y[c - 1][0:1, :]
-        scale = to_column(c_row)
-        ccol[c * rows : (c + 1) * rows, :] = scale
-        part = slice(c * rows, (c + 1) * rows)
+
+    def in_exp(i, carry):
+        sums, moments, own = carry
+        scale = to_column(crow[i])
+        part = pl.ds(pl.multiple_of(i * rows, rows), rows)
+        own_place = ahead == i * (2 * rows)
+        new_sums, new_moments = [], []
         for n in range(side):
-            row_scale = inverse_temp * (q_row if n == 0 else aux_x[n - 1][7:8, :])
             columns = slice(n * rows, (n + 1) * rows)
-            score = (si_mine[part, columns] + si_peer[part, columns]) * (scale * row_scale)
+            score = (si_mine[part, columns] + si_peer[part, columns]) * (scale * near_scale[n])
             weight = jnp.exp(score)
-            if c == 0 and n == 0:
-                own_score = jnp.sum(jnp.where(diagonal, score, 0.0), axis=0, keepdims=True)
-                weight = jnp.where(diagonal, 0.0, weight)
+            if n == 0:
+                own = own + jnp.sum(jnp.where(own_place, score, 0.0), axis=0, keepdims=True)
+                weight = jnp.where(own_place, 0.0, weight)
+            moment = weight * score
             ein_t[part, columns] = weight
-            ein_s[part, columns] = weight * score
+            ein_s[part, columns] = moment
             ein[columns, part] = jnp.transpose(weight * scale).astype(bf16)
-            in_sums[n] = in_sums[n] + jnp.sum(weight, axis=0, keepdims=True)
-            in_moments[n] = in_moments[n] + jnp.sum(weight * score, axis=0, keepdims=True)
+            new_sums.append(sums[n] + jnp.sum(weight, axis=0, keepdims=True))
+            new_moments.append(moments[n] + jnp.sum(moment, axis=0, keepdims=True))
+        return tuple(new_sums), tuple(new_moments), own
+
+    zeros = tuple(jnp.zeros((1, lanes), f32) for _ in range(side))
+    in_sums, in_moments, own_score = lax.fori_loop(0, side, in_exp, (zeros, zeros, zeros[0]))
     for n in range(1, side):
         sum_out[6 + n] = jnp.where(line == 0, in_sums[n], in_moments[n])
         send(sum_out.at[6 + n], sum_x.at[n - 1], x_homes[n - 1], "sum_x", True)
@@ -545,12 +552,16 @@
     repeat = width // lanes
 
     wait_came("fac_x", fac_x)
-    for n in range(side):
-        near_row = factor if n == 0 else fac_x[n - 1][0:1, :]
-        columns = slice(n * rows, (n + 1) * rows)
-        for c in range(side):
-            part = slice(c * rows, (c + 1) * rows)
-            ein[part, columns] = (ein_t[part, columns] * near_row).astype(bf16)
+    near_rows = [factor if n == 0 else fac_x[n - 1][0:1, :] for n in range(side)]
+
+    def in_weights(i, _):
+        part = pl.ds(pl.multiple_of(i * rows, rows), rows)
+        for n in range(side):
+            columns = slice(n * rows, (n + 1) * rows)
+            ein[part, columns] = (ein_t[part, columns] * near_rows[n]).astype(bf16)
+        return 0
+
+    lax.fori_loop(0, side, in_weights, 0)
 
     in_product(3 * rows, 4 * rows, xq)
     y_first = square_first(ys_send, ys_recv, at_y, "back_y")
@@ -579,30 +590,35 @@
 
     in_product(0, rows, xq)
 
-    own_along = None
-    for c in range(side):
-        part = slice(c * rows, (c + 1) * rows)
+    inverse_rows = [inverse if n == 0 else fac_x[n - 1][1:2, :] for n in range(side)]
+
+    def own_shares(i, _):
+        part = pl.ds(pl.multiple_of(i * rows, rows), rows)
         shares = jnp.zeros((rows, lanes), f32)
         for n in range(side):
-            inverse_row = inverse if n == 0 else fac_x[n - 1][1:2, :]
-            shares = shares + ein_s[part, n * rows : (n + 1) * rows] * inverse_row
-        row = jnp.sum(jnp.transpose(shares), axis=0, keepdims=True)
-        if c == 0:
-            own_along = row - rest * own_score * inverse
-        else:
-            own_out[c - 1] = row
-            send(own_out.at[c - 1], own_y.at[c - 1], y_homes[c - 1], "own", True)
+            shares = shares + ein_s[part, n * rows : (n + 1) * rows] * inverse_rows[n]
+        own_out[i] = jnp.sum(jnp.transpose(shares), axis=0, keepdims=True)
+        return 0
+
+    lax.fori_loop(0, side, own_shares, 0)
+    own_along = own_out[0] - rest * own_score * inverse
+    for c in range(1, side):
+        send(own_out.at[c], own_y.at[c - 1], y_homes[c - 1], "own", True)
     send_back(3, 0, half, True, came=(4, 0))
     send_back(3, half, half, False, came=(4, half))
     hard_query(0, 2, 0)
 
     wait_came("fac_z", fac_z)
-    for m in range(7):
-        columns = slice(m * rows, (m + 1) * rows)
-        tile_row = of_tile(m, lambda block: fac_z[block])
-        for c in range(tiles):
-            part = slice(c * rows, (c + 1) * rows)
-            wt[part, columns] = (eh_t[part, columns] * tile_row).astype(bf16)
+    tile_rows = [of_tile(m, lambda block: fac_z[block]) for m in range(7)]
+
+    def hard_weights(i, _):
+        part = pl.ds(pl.multiple_of(i * rows, rows), rows)
+        for m in range(7):
+            columns = slice(m * rows, (m + 1) * rows)
+            wt[part, columns] = (eh_t[part, columns] * tile_rows[m]).astype(bf16)
+        return 0
+
+    lax.fori_loop(0, tiles, hard_weights, 0)
 
     y_second += square_last(y_first, ys_send, ys_recv, at_y, "back_y")
     send_back(1, half, half, True, came=(2, half))
@@ -803,7 +819,6 @@
             f(p_rows + rows, lanes),
             f(p_rows, lanes),
             f(rows, lanes),
-            f(4 * rows, lanes),
             f(8, lanes),
             f(7, 8, lanes),
             f(3, 8, lanes),
@@ -816,7 +831,8 @@
             f(2, lanes),
             f(7, 1, lanes),
             f(3, 2, lanes),
-            f(3, 1, lanes),
+            f(4, 1, lanes),
+            f(4, 1, lanes),
             f(3, 1, lanes),
             f(8, 1, lanes),
             f(4, 1, lanes),

time: 96.6 us -> 96.6 us (level)
  no operation moved by 1% of the time
where the time goes in v5:
time: 96.6 us; the launch traced here: 94.8 us
  Pallas kernels  94.2 us (98%)
    pallas_call x1, Pallas kernels, on_device(): pl.pallas_call(kernel, out_shape=(pltpu.VMEM((8, lanes), f32), pltpu.VMEM...  92.7 us

profile of v5, /device:TPU:1, one launch (start us, length us, event | category | flops | bytes accessed | tf_op | source)
XLA Modules:
  0.0 94.8 jit_solution(9940363151281311440)
XLA Ops:
  0.6 92.7 %shard_map.76 = (f32[8,128]{1,0:T(8,128)S(1)}, bf16[128,2048]{1,0:T(8,128)(2,1)S(1)}, bf16[512,2048]{1,0:T(8,128)(2,1)S(1)}) custom-call(s32[1,128]{1,0:T(1,128)} %bitcast.6, s32[7,128]{1,0:T(8,128)} %bitcast.4, s32[7,128]{1,0:T(8,128)} %bitcast.5, bf16[128,2048]{1,0:T(8,128)(2,1)} %q_hbm.1, bf16[512,2048]{1,0:T(8,128)(2,1)} %p_hbm.1), custom_call_target="tpu_custom_call" | custom-call | flops 15000000512 | bytes 6000000 | tf_op jit(solution)/shard_map/pallas_call | solution.py:783
  93.3 1.5 %shard_map.77 = (f32[1,1]{1,0:T(1,128)}, bf16[128,2048]{1,0:T(8,128)(2,1)}, bf16[512,2048]{1,0:T(8,128)(2,1)}) custom-call(f32[8,128]{1,0:T(8,128)S(1)} %get-tuple-element.9.loss_ref, bf16[128,2048]{1,0:T(8,128)(2,1)S(1)} %get-tuple-element.10.dq_ref, bf16[512,2048]{1,0:T(8,128)(2,1)S(1)} %get-tuple-element.11.dp_ref), custom_call_target="tpu_custom_call" | custom-call | tf_op jit(solution)/shard_map/pallas_call | solution.py:857

commit v6 on v5

--- a/solution.py
+++ b/solution.py
@@ -41,14 +41,17 @@
 
 
 def kernel(
-    slot_ref,
-    offset_ref,
-    hard_slot_ref,
+    slot_hbm,
+    offset_hbm,
+    hard_slot_hbm,
     q_hbm,
     p_hbm,
     loss_ref,
     dq_ref,
     dp_ref,
+    slot_ref,
+    offset_ref,
+    hard_slot_ref,
     p_ref,
     zq,
     sh_mine,
@@ -179,15 +182,24 @@
     y_targets = [at_y(1), at_y(-1), at_y(2)]
     y_homes = [at_y(-1), at_y(1), at_y(2)]
 
-    load_q = pltpu.make_async_copy(q_hbm, xq.at[rows_of(0)], load_sems.at[0])
-    load_p = pltpu.make_async_copy(p_hbm, p_ref, load_sems.at[1])
-    load_q.start()
-    load_p.start()
-
     barrier = pltpu.get_barrier_semaphore()
     peers = z_targets + x_targets + y_targets + [other]
     for peer in peers:
         pl.semaphore_signal(barrier, inc=1, device_id=peer, device_id_type=pl.DeviceIdType.MESH)
+    loads = [
+        pltpu.make_async_copy(src, dst, load_sems.at[i])
+        for i, (src, dst) in enumerate(
+            [
+                (slot_hbm, slot_ref),
+                (offset_hbm, offset_ref),
+                (hard_slot_hbm, hard_slot_ref),
+                (p_hbm, p_ref),
+                (q_hbm, xq.at[rows_of(0)]),
+            ]
+        )
+    ]
+    for load in loads:
+        load.start()
     pl.semaphore_wait(barrier, len(peers))
 
     def z_rows(k, before, c):
@@ -202,8 +214,8 @@
         z_left[1, 1 - c] = send(left_own, zq.at[z_rows(1, False, 1 - c)], at_z(-1), "z")
     x_right = send(q_hbm, xq.at[rows_of(1)], at_x(1), "x")
     x_left = send(q_hbm, xq.at[rows_of(2)], at_x(-1), "x")
-    load_q.wait()
-    load_p.wait()
+    for load in loads:
+        load.wait()
     q_ref = xq
 
     slots = slot_ref[0:1, :]
@@ -787,9 +799,12 @@
             pltpu.VMEM(queries.shape, bf16),
             pltpu.VMEM(passages.shape, bf16),
         ),
-        in_specs=[vmem, vmem, vmem, hbm, hbm],
+        in_specs=[hbm] * 5,
         out_specs=(vmem, vmem, vmem),
         scratch_shapes=[
+            pltpu.VMEM((1, rows), jnp.int32),
+            pltpu.VMEM((7, rows), jnp.int32),
+            pltpu.VMEM((7, rows), jnp.int32),
             b(p_rows, width),
             b(9 * rows, width),
             f(7, p_rows, rows),
@@ -845,7 +860,7 @@
             f(rows, lanes),
             pltpu.SemaphoreType.DMA((len(kinds),)),
             pltpu.SemaphoreType.DMA((len(shared) + alone,)),
-            pltpu.SemaphoreType.DMA((2,)),
+            pltpu.SemaphoreType.DMA((5,)),
         ],
         compiler_params=pltpu.CompilerParams(
             collective_id=0, has_side_effects=True, vmem_limit_bytes=58 * 1024 * 1024

time: 96.6 us -> 95.9 us (level)
  no operation moved by 1% of the time
where the time goes in v6:
time: 95.9 us; the launch traced here: 94.3 us
  Pallas kernels  93.7 us (98%)
    pallas_call x1, Pallas kernels, on_device(): pl.pallas_call(kernel, out_shape=(pltpu.VMEM((8, lanes), f32), pltpu.VMEM...  92.2 us

profile of v6, /device:TPU:1, one launch (start us, length us, event | category | flops | bytes accessed | tf_op | source)
XLA Modules:
  0.0 94.3 jit_solution(13499290821926638043)
XLA Ops:
  0.6 92.2 %shard_map.76 = (f32[8,128]{1,0:T(8,128)S(1)}, bf16[128,2048]{1,0:T(8,128)(2,1)S(1)}, bf16[512,2048]{1,0:T(8,128)(2,1)S(1)}) custom-call(s32[1,128]{1,0:T(1,128)} %bitcast.6, s32[7,128]{1,0:T(8,128)} %bitcast.4, s32[7,128]{1,0:T(8,128)} %bitcast.5, bf16[128,2048]{1,0:T(8,128)(2,1)} %q_hbm.1, bf16[512,2048]{1,0:T(8,128)(2,1)} %p_hbm.1), custom_call_target="tpu_custom_call" | custom-call | flops 15000000512 | bytes 6000000 | tf_op jit(solution)/shard_map/pallas_call | solution.py:795
  92.8 1.5 %shard_map.77 = (f32[1,1]{1,0:T(1,128)}, bf16[128,2048]{1,0:T(8,128)(2,1)}, bf16[512,2048]{1,0:T(8,128)(2,1)}) custom-call(f32[8,128]{1,0:T(8,128)S(1)} %get-tuple-element.9.loss_ref, bf16[128,2048]{1,0:T(8,128)(2,1)S(1)} %get-tuple-element.10.dq_ref, bf16[512,2048]{1,0:T(8,128)(2,1)S(1)} %get-tuple-element.11.dp_ref), custom_call_target="tpu_custom_call" | custom-call | tf_op jit(solution)/shard_map/pallas_call | solution.py:872

commit v7 on v6

--- a/solution.py
+++ b/solution.py
@@ -12,7 +12,7 @@
 shared = ("aux_z", "aux_x", "aux_y", "sum_z", "sum_x", "fac_z", "fac_x", "own")
 shared = shared + ("loss_z", "loss_x", "loss_y")
 kinds = shared + ("z", "x", "y", "back_z", "back_x", "back_y", "norm", "hard", "in", "along")
-alone = 61
+alone = 68
 f32 = jnp.float32
 bf16 = jnp.bfloat16
 
@@ -275,8 +275,19 @@
     aux_own[0:7, :] = (owner_ids * p_rows + hard_slot_ref[...]).astype(f32)
     aux_own[7:8, :] = q_row
     pos_own[...] = position_row
-    for m in range(7):
-        send(aux_own, aux_z.at[m], z_targets[m], "aux_z", True)
+    aux_copies = [
+        send(aux_own, aux_z.at[0], at_z(1), "aux_z"),
+        send(aux_own, aux_z.at[1], at_z(-1), "aux_z"),
+    ]
+
+    def forward_aux(blocks):
+        for m in blocks:
+            aux_copies[m].wait_recv()
+            if m < 5:
+                aux_copies.append(
+                    send(aux_z.at[m], aux_z.at[m + 2], at_z(-1 if m % 2 else 1), "aux_z")
+                )
+
     for m in range(3):
         send(aux_own, aux_x.at[m], x_targets[m], "aux_x", True)
         send(pos_own, aux_y.at[m], y_targets[m], "aux_y", True)
@@ -314,8 +325,6 @@
     def hard_exp(tile):
         if hard_copies[tile] is not None:
             hard_copies[tile].wait_recv()
-        if tile == 0:
-            wait_came("aux_z", aux_z)
         packet = of_tile(tile, lambda block: aux_z[block])
         row_scale = inverse_temp * packet[7:8, :]
         columns = slice(tile * rows, (tile + 1) * rows)
@@ -348,7 +357,9 @@
         send(sum_out.at[slot], sum_z.at[slot], z_homes[slot], "sum_z", True)
 
     forward_z(1, 0)
+    forward_aux((0, 1))
     forward_z(1, 1)
+    forward_aux((2, 3))
     x_right.wait_recv()
     x_far_right = send(xq.at[rows_of(1, 0)], xq.at[rows_of(3, 0)], at_x(1), "x")
     x_left.wait_recv()
@@ -361,6 +372,7 @@
     hard_exp(0)
     hard_exp(1)
     forward_z(2, 0)
+    forward_aux((4, 5))
 
     x_far_right.wait_recv()
     x_far_left.wait_recv()
@@ -414,6 +426,7 @@
         send(sum_out.at[6 + n], sum_x.at[n - 1], x_homes[n - 1], "sum_x", True)
 
     forward_z(2, 1)
+    forward_aux((6,))
 
     def in_product(start, stop, other_rows):
         def body(i, _):

time: 95.9 us -> 100 us (1.043)
  Pallas kernels: 93.7 us -> 98.5 us
    pallas_call x1, Pallas kernels: 92.2 us -> 97 us  [on_device(): pl.pallas_call(kernel, out_shape=(pltpu.VMEM((8, lanes), f32), pltpu.VMEM...]
where the time goes in v7:
time: 100 us; the launch traced here: 99.2 us
  Pallas kernels  98.5 us (98%)
    pallas_call x1, Pallas kernels, on_device(): pl.pallas_call(kernel, out_shape=(pltpu.VMEM((8, lanes), f32), pltpu.VMEM...  97 us

profile of v7, /device:TPU:1, one launch (start us, length us, event | category | flops | bytes accessed | tf_op | source)
XLA Modules:
  0.0 99.2 jit_solution(10779736483060215139)
XLA Ops:
  0.6 97.0 %shard_map.76 = (f32[8,128]{1,0:T(8,128)S(1)}, bf16[128,2048]{1,0:T(8,128)(2,1)S(1)}, bf16[512,2048]{1,0:T(8,128)(2,1)S(1)}) custom-call(s32[1,128]{1,0:T(1,128)} %bitcast.6, s32[7,128]{1,0:T(8,128)} %bitcast.4, s32[7,128]{1,0:T(8,128)} %bitcast.5, bf16[128,2048]{1,0:T(8,128)(2,1)} %q_hbm.1, bf16[512,2048]{1,0:T(8,128)(2,1)} %p_hbm.1), custom_call_target="tpu_custom_call" | custom-call | flops 15000000512 | bytes 6000000 | tf_op jit(solution)/shard_map/pallas_call | solution.py:808
  97.7 1.5 %shard_map.77 = (f32[1,1]{1,0:T(1,128)}, bf16[128,2048]{1,0:T(8,128)(2,1)}, bf16[512,2048]{1,0:T(8,128)(2,1)}) custom-call(f32[8,128]{1,0:T(8,128)S(1)} %get-tuple-element.9.loss_ref, bf16[128,2048]{1,0:T(8,128)(2,1)S(1)} %get-tuple-element.10.dq_ref, bf16[512,2048]{1,0:T(8,128)(2,1)S(1)} %get-tuple-element.11.dp_ref), custom_call_target="tpu_custom_call" | custom-call | tf_op jit(solution)/shard_map/pallas_call | solution.py:885
